TPU v7x, 128 devices: a whole 4x4x4 slice. The times are simulated.
128 devices in a mesh: replica: 32 (over y, z, core), tensor: 4 (over x).
Axes of the slice: x: 4, y: 4, z: 4, core: 2. Of those that a mesh axis runs over, the one named last changes fastest.
Arguments:
- hidden_in: bfloat16 [4, 1024, 5120], P(None, 'replica'), may hold values from -600 to 600
- norm_gain: float32 [5120], replicated, may hold values from 0.1 to 1.9
- w_query: bfloat16 [5120, 2560], P(None, 'tensor'), may hold values from -0.078125 to 0.078125
- w_key: bfloat16 [5120, 512], P(None, 'tensor'), may hold values from -0.078125 to 0.078125
- w_value: bfloat16 [5120, 512], P(None, 'tensor'), may hold values from -0.078125 to 0.078125
- w_out: bfloat16 [2560, 5120], P('tensor'), may hold values from -0.25 to 0.25
- kv_pages: bfloat16 [4096, 2, 128, 512], P('replica', None, None, 'tensor'), may hold values from -210 to 210
- lengths: int32 [1024], P('replica'), may hold values from 1 to 512, as said below
- page_table: int32 [1024, 4], P('replica'), may hold values from 0 to 127, as said below
- destination: int32 [1024], P('replica'), may hold values from 0 to 31, as said below
Outputs:
- attended: bfloat16 [4, 1024, 5120], P(None, 'replica')
Inputs may be any that keep to these rules, and one draw needn't show every extreme that they name: `lengths`: some trajectory has exactly 512 cached tokens. `page_table`: the 4 entries of a row are distinct local page numbers of its replica's pool of 128 pages; no two rows of a replica share a page. `destination`: each replica sends exactly one of its rows to each replica (itself included), and each replica receives exactly one row for each slot b % 32.
All inputs are finite; a program needn't handle non-finite values.
Results may differ from a plain program's by a relative error of at most 0.01.
The roundings to bfloat16 on the way count: a program that leaves them out, or rounds other values in their place, can miss the bound.
Values may be sent and summed in bfloat16 or wider, within the bound.
A program may use at most 128 MiB of HBM per device.

v0:
```python
import math

import jax
import jax.numpy as jnp
from jax import lax
from jax.sharding import PartitionSpec as P

HD = 128


ROPE_BASE = 1000000.0
EPSILON = 1e-06


def rotate(vectors, positions):
    half_dim = vectors.shape[-1] // 2
    inv_freq = ROPE_BASE ** (-(jnp.arange(half_dim, dtype=jnp.float32) * (2.0 / vectors.shape[-1])))
    angles = positions.astype(jnp.float32)[..., None] * inv_freq
    cosine = jnp.cos(angles)
    sine = jnp.sin(angles)
    first_half = vectors[..., :half_dim]
    second_half = vectors[..., half_dim:]
    return jnp.concatenate(
        [first_half * cosine - second_half * sine, second_half * cosine + first_half * sine], -1
    )


def softmax_part(scores, inside):
    scores = jnp.where(inside, scores, -jnp.inf)
    peak = jnp.max(scores, -1)
    weights = jnp.exp(scores - peak[..., None]).astype(jnp.bfloat16)
    weight_sum = jnp.sum(weights, -1, dtype=jnp.float32)
    return (weights, peak, weight_sum)


def cached_part(asked, cache, row_lengths, kv_heads):
    row_count, step_count, columns = asked.shape
    head_dim = cache.shape[-1] // kv_heads
    group_size = columns // (kv_heads * head_dim)
    span = cache.shape[1] * cache.shape[3]
    cache_keys = cache[:, :, 0].reshape(row_count, span, kv_heads, head_dim)
    cache_values = cache[:, :, 1].reshape(row_count, span, kv_heads, head_dim)
    grouped = asked.reshape(row_count, step_count, kv_heads, group_size, head_dim)
    scores = jnp.einsum(
        "nsghd,ntgd->nsght", grouped, cache_keys, preferred_element_type=jnp.float32
    ) / math.sqrt(head_dim)
    inside = jnp.arange(span)[None, :] < row_lengths[:, None]
    weights, peak, weight_sum = softmax_part(scores, inside[:, None, None, None, :])
    blended = jnp.einsum(
        "nsght,ntgd->nsghd", weights, cache_values, preferred_element_type=jnp.float32
    )
    head_total = kv_heads * group_size
    return (
        blended.reshape(row_count, step_count, columns),
        peak.reshape(row_count, step_count, head_total),
        weight_sum.reshape(row_count, step_count, head_total),
    )


def shards(
    hidden_in, norm_gain, w_query, w_key, w_value, w_out, kv_pages, lengths, page_table, destination
):
    step_count, rows_here, model_width = hidden_in.shape
    replicas = lax.axis_size("replica")
    kv_heads = w_key.shape[1] // HD
    q_heads = w_query.shape[1] // HD
    group_size = q_heads // kv_heads
    widened = hidden_in.astype(jnp.float32)
    scale = lax.rsqrt(jnp.mean(widened * widened, -1, keepdims=True) + EPSILON)
    normed = (
        (widened * scale * norm_gain)
        .astype(jnp.bfloat16)
        .reshape(step_count * rows_here, model_width)
    )
    query_raw = (
        jnp.dot(normed, w_query, preferred_element_type=jnp.float32)
        .reshape(step_count, rows_here, q_heads, HD)
        .transpose(1, 0, 2, 3)
    )
    key_raw = (
        jnp.dot(normed, w_key, preferred_element_type=jnp.float32)
        .reshape(step_count, rows_here, kv_heads, HD)
        .transpose(1, 0, 2, 3)
    )
    value_raw = (
        jnp.dot(normed, w_value, preferred_element_type=jnp.float32)
        .reshape(step_count, rows_here, kv_heads, HD)
        .transpose(1, 0, 2, 3)
    )
    own_rows = jnp.arange(rows_here, dtype=jnp.int32)
    slot_of_dst = jnp.zeros((replicas,), jnp.int32).at[destination].set(own_rows)
    outgoing = jnp.stack([slot_of_dst, lengths[slot_of_dst]], -1)
    sent_cache = kv_pages[page_table[slot_of_dst]]
    moved, arrived = (
        lax.all_to_all(sent_cache, "replica", split_axis=0, concat_axis=0, tiled=True),
        lax.all_to_all(outgoing, "replica", split_axis=0, concat_axis=0, tiled=True),
    )
    source_slot = arrived[:, 0]
    source_of_slot = (
        jnp.zeros((rows_here,), jnp.int32)
        .at[source_slot]
        .set(jnp.arange(replicas, dtype=jnp.int32))
    )
    slot_length = arrived[source_of_slot, 1]
    positions = slot_length[:, None, None] + jnp.arange(step_count, dtype=jnp.int32)[None, :, None]
    queries = rotate(query_raw, positions).astype(jnp.bfloat16)
    fresh_keys = rotate(key_raw, positions).astype(jnp.bfloat16)
    fresh_values = value_raw.astype(jnp.bfloat16)
    by_source = queries.reshape(rows_here, step_count, q_heads * HD)[source_slot]
    cache_out, cache_peak, cache_sum = cached_part(by_source, moved, arrived[:, 1], kv_heads)
    cache_out = cache_out[source_of_slot].reshape(rows_here, step_count, q_heads, HD)
    cache_peak = cache_peak[source_of_slot]
    cache_sum = cache_sum[source_of_slot]
    grouped = queries.reshape(rows_here, step_count, kv_heads, group_size, HD)
    scores = jnp.einsum(
        "rsghd,rjgd->rsghj", grouped, fresh_keys, preferred_element_type=jnp.float32
    ) / math.sqrt(HD)
    causal = jnp.arange(step_count)[:, None] >= jnp.arange(step_count)[None, :]
    weights, fresh_peak, fresh_sum = softmax_part(scores, causal[None, :, None, None, :])
    fresh_out = jnp.einsum(
        "rsghj,rjgd->rsghd", weights, fresh_values, preferred_element_type=jnp.float32
    )
    fresh_out = fresh_out.reshape(rows_here, step_count, q_heads, HD)
    fresh_peak = fresh_peak.reshape(rows_here, step_count, q_heads)
    fresh_sum = fresh_sum.reshape(rows_here, step_count, q_heads)
    highest = jnp.maximum(cache_peak, fresh_peak)
    factor_c = jnp.exp(cache_peak - highest)
    factor_f = jnp.exp(fresh_peak - highest)
    blended = (cache_out * factor_c[..., None] + fresh_out * factor_f[..., None]) / (
        cache_sum * factor_c + fresh_sum * factor_f
    )[..., None]
    heads = blended.reshape(rows_here, step_count, q_heads * HD).astype(jnp.bfloat16)
    flat_heads = heads.transpose(1, 0, 2).reshape(step_count * rows_here, q_heads * HD)
    partial_out = jnp.dot(flat_heads, w_out, preferred_element_type=jnp.float32)
    summed = lax.psum(partial_out, "tensor").astype(jnp.bfloat16)
    return summed.reshape(step_count, rows_here, model_width)


def solution(mesh):
    in_specs = (
        P(None, "replica", None),
        P(),
        P(None, "tensor"),
        P(None, "tensor"),
        P(None, "tensor"),
        P("tensor", None),
        P("replica", None, None, "tensor"),
        P("replica"),
        P("replica", None),
        P("replica"),
    )
    out_specs = P(None, "replica", None)
    return jax.shard_map(shards, mesh=mesh, in_specs=in_specs, out_specs=out_specs, check_vma=False)
```

profile of v0, /device:TPU:32, one launch (start us, length us, event | category | flops | bytes accessed | tf_op | source)
XLA Modules:
  0.0 234.5 jit_solution(12032596597751196254)
XLA Ops:
  0.0 0.8 compare_select_fusion.4
  0.8 0.7 scatter_custom_fusion
  1.5 1.4 gather_fusion.2
  2.8 0.7 copy.157
  3.5 8.2 %all-to-all-start.1 = ((s32[32,1,2]{2,1,0:T(1,128)}), s32[32,1,2]{2,1,0:T(1,128)S(1)}, u32[]{:S(2)}, u32[]{:S(2)}) async-start(s32[32,1,2]{2,1,0:T(1,128)} %copy.157), calls=%async_computation.1 | async-start | bytes 32768 | tf_op jit(solution)/shard_map/all_to_all | solution.py:96
  11.8 0.8 copy.153
  12.5 0.6 gather_fusion
  13.3 0.1 reshape.271
  13.4 9.9 %gather_fusion.1 = bf16[128,2,128,128]{3,2,1,0:T(8,128)(2,1)} fusion(bf16[128,2,128,128]{3,2,1,0:T(8,128)(2,1)} %param.16, s32[1024]{0:T(1024)S(1)} %pad_clamp_fusion.2), kind=kCustom, calls=%fused_computation.1 | custom fusion | bytes 16777728 | tf_op jit(solution)/shard_map/gather | solution.py:93
  23.4 10.3 %copy.156 = bf16[32,4,2,128,128]{4,3,1,2,0:T(8,128)(2,1)} copy(bf16[32,4,2,128,128]{4,3,2,1,0:T(8,128)(2,1)} %bitcast.133) | data formatting | bytes 16777216 | tf_op jit(solution)/shard_map/gather | solution.py:93
  33.7 7.4 %all-to-all-start = ((bf16[32,4,2,128,128]{4,3,1,2,0:T(8,128)(2,1)}), bf16[32,4,2,128,128]{4,3,1,2,0:T(8,128)(2,1)}, u32[]{:S(2)}, u32[]{:S(2)}) async-start(bf16[32,4,2,128,128]{4,3,1,2,0:T(8,128)(2,1)} %copy.156), calls=%async_computation | async-start | bytes 16777216 | tf_op jit(solution)/shard_map/all_to_all | solution.py:95
  41.2 9.6 %copy.159 = bf16[5120,640]{0,1:T(8,128)(2,1)} copy(bf16[5120,640]{1,0:T(8,128)(2,1)} %param.12) | data formatting | bytes 13107200 | tf_op args[2]
  50.8 0.4 fusion
  51.2 0.6 fusion.15
  51.8 0.3 copy-done.4
  52.1 0.6 fusion.21
  52.7 1.5 copy-done.2
  54.1 2.2 fusion.11
  56.4 0.9 scatter_custom_fusion.1
  57.3 0.8 gather_fusion.3
  58.1 0.3 multiply_cosine_fusion.1
  58.4 0.2 multiply_subtract_fusion
  58.6 0.1 maximum_convert_fusion
  58.8 0.1 reshape.362
  58.9 0.7 gather_fusion.4
  59.7 0.3 fusion.44
  60.1 1.3 fusion.57
  61.6 0.3 convert_reduce_fusion.1
  61.9 0.3 convolution_bitcast_fusion
  62.2 0.1 reshape.365
  62.5 102.9 %all-to-all-done = bf16[32,4,2,128,128]{4,3,1,2,0:T(8,128)(2,1)} async-done(((bf16[32,4,2,128,128]{4,3,1,2,0:T(8,128)(2,1)}), bf16[32,4,2,128,128]{4,3,1,2,0:T(8,128)(2,1)}, u32[]{:S(2)}, u32[]{:S(2)}) %all-to-all-start) | async-done | bytes 8388640 | tf_op jit(solution)/shard_map/all_to_all | solution.py:95
  165.4 4.0 %fusion.56 = (bf16[32,4,1,128,128]{4,3,1,2,0:T(8,128)(2,1)S(1)}, bf16[32,4,1,128,128]{4,3,1,2,0:T(8,128)(2,1)S(1)}) fusion(bf16[32,4,2,128,128]{4,3,1,2,0:T(8,128)(2,1)} %all-to-all-done), kind=kLoop, calls=%fused_computation.93 | loop fusion | bytes 16777216 | tf_op jit(solution)/shard_map/slice | solution.py:42
  169.4 1.6 bitcast_reduce_fusion
  171.0 0.9 convert_reduce_fusion
  171.9 0.9 convolution_bitcast_fusion.1
  172.8 0.1 reshape.364
  173.0 0.6 gather_fusion.6
  173.6 0.8 gather_fusion.5
  174.3 0.6 gather_fusion.7
  175.0 0.1 copy.170
  175.2 0.1 copy.179
  175.3 0.2 div.44
  175.6 0.1 copy.171
  175.7 0.2 mul.167
  176.0 0.1 copy.176
  176.1 0.2 mul.170
  176.5 5.7 %fusion.58 = f32[128,5120]{1,0:T(8,128)} fusion(bf16[128,640]{1,0:T(8,128)(2,1)S(1)} %bitcast.137, bf16[640,5120]{1,0:T(8,128)(2,1)} %param.15), kind=kOutput, calls=%fused_computation.95 | convolution fusion | flops 838860800 | bytes 9338880 | tf_op jit(solution)/shard_map/dot_general | solution.py:134
  182.2 52.3 %all-reduce.2 = bf16[128,5120]{1,0:T(8,128)(2,1)} all-reduce(f32[128,5120]{1,0:T(8,128)} %fusion.58), channel_id=1, replica_groups=mesh['replica'=32,'tensor'=4] {'tensor'}, use_global_device_ids=true, to_apply=%region_7.8 | all-reduce | flops 655360 | bytes 3932160 | tf_op jit(solution)/shard_map/psum | solution.py:135
  (41 shorter events, 1.4 us)
Async XLA Ops:
  0.0 51.2 %copy-start = (bf16[5120,128]{1,0:T(8,128)(2,1)S(1)}, bf16[5120,128]{1,0:T(8,128)(2,1)}, u32[]{:S(2)}) copy-start(bf16[5120,128]{1,0:T(8,128)(2,1)} %param.13) | copy-start | bytes 3932164
  3.5 30.1 %all-to-all-start.1 = ((s32[32,1,2]{2,1,0:T(1,128)}), s32[32,1,2]{2,1,0:T(1,128)S(1)}, u32[]{:S(2)}, u32[]{:S(2)}) async-start(s32[32,1,2]{2,1,0:T(1,128)} %copy.157), calls=%async_computation.1 | async-start | bytes 32768 | tf_op jit(solution)/shard_map/all_to_all | solution.py:96
  33.7 131.7 %all-to-all-start = ((bf16[32,4,2,128,128]{4,3,1,2,0:T(8,128)(2,1)}), bf16[32,4,2,128,128]{4,3,1,2,0:T(8,128)(2,1)}, u32[]{:S(2)}, u32[]{:S(2)}) async-start(bf16[32,4,2,128,128]{4,3,1,2,0:T(8,128)(2,1)} %copy.156), calls=%async_computation | async-start | bytes 16777216 | tf_op jit(solution)/shard_map/all_to_all | solution.py:95
  41.1 9.7 %copy-start.3 = (bf16[4,32,5120]{2,1,0:T(8,128)(2,1)S(1)}, bf16[4,32,5120]{2,1,0:T(8,128)(2,1)}, u32[]{:S(2)}) copy-start(bf16[4,32,5120]{2,1,0:T(8,128)(2,1)} %param.10) | copy-start | bytes 3932164
  41.1 10.0 %copy-start.5 = (f32[5120]{0:T(1024)S(1)}, f32[5120]{0:T(1024)}, u32[]{:S(2)}) copy-start(f32[5120]{0:T(1024)} %param.11) | copy-start | bytes 61444
  50.8 1.3 copy-start.4
  51.2 3.0 %copy-start.2 = (bf16[5120,640]{0,1:T(8,128)(2,1)S(1)}, bf16[5120,640]{0,1:T(8,128)(2,1)}, u32[]{:S(2)}) copy-start(bf16[5120,640]{0,1:T(8,128)(2,1)} %copy.159) | copy-start | bytes 19660804
  176.5 58.0 %copy-start.1 = (bf16[5120,128]{1,0:T(8,128)(2,1)S(1)}, bf16[5120,128]{1,0:T(8,128)(2,1)}, u32[]{:S(2)}) copy-start(bf16[5120,128]{1,0:T(8,128)(2,1)} %param.13) | copy-start | bytes 3932164
where the time goes:
time: 235 us
  waiting for transfers between devices  103 us (44%)
  blocking collectives  52.3 us (22%)
  local copies, waits for them, and re-layouts  46.6 us (20%)
  starting transfers between devices  15.6 us (7%)
  matrix products  13.2 us (6%)
  other arithmetic  3.56 us (2%)
    all_to_all x1, waiting for transfers between devices, shards(): lax.all_to_all(sent_cache, 'replica', split_axis=0, concat_axis=0, tiled=...  103 us
    psum x1, blocking collectives, shards(): summed = lax.psum(partial_out, 'tensor').astype(jnp.bfloat16)  52.3 us
    gather x4, local copies, waits for them, and re-layouts, shards(): sent_cache = kv_pages[page_table[slot_of_dst]]  20.9 us
    unnamed x14, local copies, waits for them, and re-layouts  12.2 us
    all_to_all x1, starting transfers between devices, shards(): lax.all_to_all(outgoing, 'replica', split_axis=0, concat_axis=0, tiled=True)  8.21 us
    all_to_all x1, starting transfers between devices, shards(): lax.all_to_all(sent_cache, 'replica', split_axis=0, concat_axis=0, tiled=...  7.44 us
    dot_general x1, matrix products, shards(): partial_out = jnp.dot(flat_heads, w_out, preferred_element_type=jnp.float32)  5.73 us
  transfers between devices with their start and end apart: 2, of which 1 were waited for; matrix products, arithmetic and copies ran while one was open for 18% of the time, Pallas kernels for 0%

commit v1 on v0

--- a/solution.py
+++ b/solution.py
@@ -88,29 +88,29 @@
         .transpose(1, 0, 2, 3)
     )
     own_rows = jnp.arange(rows_here, dtype=jnp.int32)
-    slot_of_dst = jnp.zeros((replicas,), jnp.int32).at[destination].set(own_rows)
-    outgoing = jnp.stack([slot_of_dst, lengths[slot_of_dst]], -1)
-    sent_cache = kv_pages[page_table[slot_of_dst]]
-    moved, arrived = (
-        lax.all_to_all(sent_cache, "replica", split_axis=0, concat_axis=0, tiled=True),
-        lax.all_to_all(outgoing, "replica", split_axis=0, concat_axis=0, tiled=True),
-    )
+    picked = destination[None, :] == jnp.arange(replicas, dtype=jnp.int32)[:, None]
+    slot_of_dst = jnp.sum(jnp.where(picked, own_rows[None, :], 0), 1)
+    own_lengths = jnp.sum(jnp.where(picked, lengths[None, :], 0), 1)
+    outgoing = jnp.stack([slot_of_dst, own_lengths], -1)
+    arrived = lax.all_to_all(outgoing, "replica", split_axis=0, concat_axis=0, tiled=True)
     source_slot = arrived[:, 0]
-    source_of_slot = (
-        jnp.zeros((rows_here,), jnp.int32)
-        .at[source_slot]
-        .set(jnp.arange(replicas, dtype=jnp.int32))
-    )
-    slot_length = arrived[source_of_slot, 1]
+    slot_match = source_slot[:, None] == own_rows[None, :]
+    source_of_slot = jnp.sum(jnp.where(slot_match, own_rows[:, None], 0), 0)
+    slot_length = jnp.sum(jnp.where(slot_match, arrived[:, 1:2], 0), 0)
     positions = slot_length[:, None, None] + jnp.arange(step_count, dtype=jnp.int32)[None, :, None]
     queries = rotate(query_raw, positions).astype(jnp.bfloat16)
     fresh_keys = rotate(key_raw, positions).astype(jnp.bfloat16)
     fresh_values = value_raw.astype(jnp.bfloat16)
-    by_source = queries.reshape(rows_here, step_count, q_heads * HD)[source_slot]
-    cache_out, cache_peak, cache_sum = cached_part(by_source, moved, arrived[:, 1], kv_heads)
-    cache_out = cache_out[source_of_slot].reshape(rows_here, step_count, q_heads, HD)
-    cache_peak = cache_peak[source_of_slot]
-    cache_sum = cache_sum[source_of_slot]
+    package = jnp.concatenate([queries, fresh_keys, fresh_values], 2)[source_slot]
+    package = lax.all_to_all(package, "replica", split_axis=0, concat_axis=0, tiled=True)
+    queries = package[:, :, :q_heads]
+    fresh_keys = package[:, :, q_heads : q_heads + kv_heads]
+    fresh_values = package[:, :, q_heads + kv_heads :]
+    cache = kv_pages[page_table[slot_of_dst]]
+    cache_out, cache_peak, cache_sum = cached_part(
+        queries.reshape(rows_here, step_count, q_heads * HD), cache, own_lengths, kv_heads
+    )
+    cache_out = cache_out.reshape(rows_here, step_count, q_heads, HD)
     grouped = queries.reshape(rows_here, step_count, kv_heads, group_size, HD)
     scores = jnp.einsum(
         "rsghd,rjgd->rsghj", grouped, fresh_keys, preferred_element_type=jnp.float32
@@ -130,6 +130,8 @@
         cache_sum * factor_c + fresh_sum * factor_f
     )[..., None]
     heads = blended.reshape(rows_here, step_count, q_heads * HD).astype(jnp.bfloat16)
+    heads = lax.all_to_all(heads, "replica", split_axis=0, concat_axis=0, tiled=True)
+    heads = heads[source_of_slot]
     flat_heads = heads.transpose(1, 0, 2).reshape(step_count * rows_here, q_heads * HD)
     partial_out = jnp.dot(flat_heads, w_out, preferred_element_type=jnp.float32)
     summed = lax.psum(partial_out, "tensor").astype(jnp.bfloat16)

time: 235 us -> 155 us (0.66)
  the two profiles are of different devices: /device:TPU:32 before, /device:TPU:0 now
where the time goes in v1:
time: 155 us; the launch traced here: 154 us
  blocking collectives  53.4 us (34%)
  local copies, waits for them, and re-layouts  36.3 us (23%)
  matrix products  22 us (14%)
  starting transfers between devices  19.8 us (13%)
  waiting for transfers between devices  16.5 us (11%)
  other arithmetic  6.1 us (4%)
    psum x1, blocking collectives, shards(): summed = lax.psum(partial_out, 'tensor').astype(jnp.bfloat16)  53.4 us
    unnamed x20, local copies, waits for them, and re-layouts  11.2 us
    gather x3, local copies, waits for them, and re-layouts, shards(): cache = kv_pages[page_table[slot_of_dst]]  10.6 us
    all_to_all x1, starting transfers between devices, shards(): lax.all_to_all(outgoing, 'replica', split_axis=0, concat_axis=0, tiled=True)  8.42 us
    all_to_all x1, waiting for transfers between devices, shards(): lax.all_to_all(package, 'replica', split_axis=0, concat_axis=0, tiled=True)  8.38 us
    all_to_all x1, waiting for transfers between devices, shards(): lax.all_to_all(heads, 'replica', split_axis=0, concat_axis=0, tiled=True)  8.09 us
    all_to_all x1, starting transfers between devices, shards(): lax.all_to_all(package, 'replica', split_axis=0, concat_axis=0, tiled=True)  7.57 us
    slice x1, local copies, waits for them, and re-layouts, cached_part(): cache_values = cache[:, :, 1].reshape(row_count, span, kv_heads, head_dim)  6.04 us
  transfers between devices with their start and end apart: 3, of which 2 were waited for; matrix products, arithmetic and copies ran while one was open for 23% of the time, Pallas kernels for 0%

profile of v1, /device:TPU:0, one launch (start us, length us, event | category | flops | bytes accessed | tf_op | source)
XLA Modules:
  0.0 154.3 jit_solution(16581932719264741556)
XLA Ops:
  0.0 0.9 select_reduce_fusion.3
  0.9 0.7 copy.136
  1.6 8.4 %all-to-all-start = ((s32[32,1,2]{2,1,0:T(1,128)}), s32[32,1,2]{2,1,0:T(1,128)S(1)}, u32[]{:S(2)}, u32[]{:S(2)}) async-start(s32[32,1,2]{2,1,0:T(1,128)} %copy.136), calls=%async_computation | async-start | bytes 32768 | tf_op jit(solution)/shard_map/all_to_all | solution.py:95
  10.1 1.7 %fusion = f32[4,32]{1,0:T(4,128)S(1)} fusion(bf16[4,32,5120]{2,1,0:T(8,128)(2,1)} %param.10), kind=kLoop, calls=%fused_computation.6 | loop fusion | flops 1965952 | bytes 1311232 | tf_op jit(solution)/shard_map/reduce_sum | solution.py:69
  11.7 9.7 %copy.135 = bf16[5120,640]{0,1:T(8,128)(2,1)} copy(bf16[5120,640]{1,0:T(8,128)(2,1)} %param.12) | data formatting | bytes 13107200 | tf_op args[2]
  21.5 5.0 %fusion.11 = f32[32,4,5,128]{3,0,2,1:T(8,128)S(1)} fusion(bf16[5,128,5120,1]{2,1,0,3:T(8,128)(2,1)} %bitcast.142, bf16[4,32,5120]{2,1,0:T(8,128)(2,1)S(1)} %copy-done.1, f32[5120]{0:T(1024)S(1)} %copy-done.8, f32[4,32]{1,0:T(4,128)S(1)} %add_rsqrt_fusion), kind=kOutput, calls=%fused_computation.23 | convolution fusion | flops 841482240 | bytes 8212992 | tf_op jit(solution)/shard_map/dot_general | solution.py:76
  26.5 0.6 fusion.15
  27.1 0.7 copy-done.7
  27.8 0.6 fusion.21
  28.6 0.6 gather_fusion
  29.3 0.1 reshape.302
  29.4 10.0 %gather_fusion.1 = bf16[128,2,128,128]{3,2,1,0:T(8,128)(2,1)} fusion(bf16[128,2,128,128]{3,2,1,0:T(8,128)(2,1)} %param.16, s32[1024]{0:T(1024)S(1)} %pad_clamp_fusion.2), kind=kCustom, calls=%fused_computation.1 | custom fusion | bytes 16777728 | tf_op jit(solution)/shard_map/gather | solution.py:109
  39.4 6.0 %fusion.54 = (bf16[32,4,1,128,128]{4,3,2,1,0:T(8,128)(2,1)}, bf16[32,4,1,128,128]{4,3,2,1,0:T(8,128)(2,1)}) fusion(bf16[32,4,2,128,128]{4,3,2,1,0:T(8,128)(2,1)} %bitcast.140), kind=kLoop, calls=%fused_computation.91 | loop fusion | bytes 16777216 | tf_op jit(solution)/shard_map/slice | solution.py:42
  45.4 0.6 iota_compare_fusion.3
  46.1 0.6 select_reduce_fusion
  46.7 0.3 multiply_cosine_fusion.1
  47.1 0.3 fusion.41
  47.4 0.2 subtract_convert_fusion
  47.6 0.1 pad_maximum_fusion
  47.7 0.1 copy.138
  47.8 1.4 gather_fusion.2
  49.3 7.6 %all-to-all-start.1 = ((bf16[32,4,7,128]{3,1,2,0:T(4,128)(2,1)}), bf16[32,4,7,128]{3,1,2,0:T(4,128)(2,1)S(1)}, u32[]{:S(2)}, u32[]{:S(2)}) async-start(bf16[32,4,7,128]{3,1,2,0:T(4,128)(2,1)} %gather_fusion.2), calls=%async_computation.1 | async-start | bytes 458752 | tf_op jit(solution)/shard_map/all_to_all | solution.py:105
  56.9 8.4 %all-to-all-done.1 = bf16[32,4,7,128]{3,1,2,0:T(4,128)(2,1)S(1)} async-done(((bf16[32,4,7,128]{3,1,2,0:T(4,128)(2,1)}), bf16[32,4,7,128]{3,1,2,0:T(4,128)(2,1)S(1)}, u32[]{:S(2)}, u32[]{:S(2)}) %all-to-all-start.1) | async-done | bytes 229408 | tf_op jit(solution)/shard_map/all_to_all | solution.py:105
  65.4 0.6 copy-done.3
  66.0 3.8 %bitcast_reduce_fusion = (f32[32,4,5]{2,1,0:T(4,128)S(1)}, f32[32,512,4,5]{1,3,2,0:T(8,128)S(1)}) fusion(pred[32,512]{1,0:T(8,128)(4,1)S(1)} %iota_compare_fusion, bf16[32,512,128,1]{2,1,3,0:T(8,128)(2,1)} %bitcast.141, bf16[32,4,5,128]{3,1,2,0:T(4,128)(2,1)S(1)} %slice.58), kind=kOutput, calls=%fused_computation.10 | convolution fusion | flops 84868480 | bytes 5687808 | tf_op jit(solution)/shard_map/nsghd,ntgd->nsght/dot_general | solution.py:44
  69.8 0.7 copy.145
  70.5 0.9 convert_reduce_fusion
  71.3 3.9 %convolution_bitcast_fusion.1 = f32[32,4,1,5,128]{4,3,1,0,2:T(8,128)} fusion(bf16[32,512,128,1]{2,1,3,0:T(8,128)(2,1)} %bitcast.143, f32[32,512,4,5]{1,3,2,0:T(8,128)S(1)} %get-tuple-element.28, f32[32,4,5]{2,1,0:T(4,128)S(1)} %get-tuple-element.27, pred[32,512]{1,0:T(8,128)(4,1)S(1)} %iota_compare_fusion), kind=kOutput, calls=%fused_computation.22 | convolution fusion | flops 85196800 | bytes 5851648 | tf_op jit(solution)/shard_map/nsght,ntgd->nsghd/dot_general | solution.py:49
  75.2 1.2 reshape.333
  76.4 0.1 copy.152
  76.5 0.8 fusion.55
  77.3 2.2 %fusion.56 = (f32[32,4,5]{2,1,0:T(4,128)S(1)}, f32[32,4,1,5,4]{3,4,1,0,2:T(4,128)S(1)}) fusion(bf16[32,4,5,128]{3,1,2,0:T(4,128)(2,1)} %copy-done.2, bf16[32,4,128,1]{2,0,1,3:T(8,128)(2,1)S(1)} %get-tuple-element.30, pred[4,4]{1,0:T(4,128)(4,1)} %iota_compare_fusion.3), kind=kOutput, calls=%fused_computation.93 | convolution fusion | flops 662400 | bytes 209424 | tf_op jit(solution)/shard_map/rsghd,rjgd->rsghj/dot_general | solution.py:115
  79.7 0.3 convert_reduce_fusion.1
  79.9 0.1 copy.153
  80.0 0.1 copy.154
  80.2 0.2 div.44
  80.5 0.1 copy.146
  80.6 0.2 mul.167
  80.9 0.1 copy.151
  81.0 0.2 mul.170
  81.3 0.3 convolution_bitcast_fusion
  81.6 0.1 reshape.334
  81.9 0.8 copy.155
  82.6 3.9 %all-to-all-start.2 = ((bf16[32,4,640]{2,1,0:T(4,128)(2,1)}), bf16[32,4,640]{2,1,0:T(4,128)(2,1)S(1)}, u32[]{:S(2)}, u32[]{:S(2)}) async-start(bf16[32,4,640]{2,1,0:T(4,128)(2,1)} %copy.155), calls=%async_computation.2 | async-start | bytes 327680 | tf_op jit(solution)/shard_map/all_to_all | solution.py:133
  86.5 8.1 %all-to-all-done.2 = bf16[32,4,640]{2,1,0:T(4,128)(2,1)S(1)} async-done(((bf16[32,4,640]{2,1,0:T(4,128)(2,1)}), bf16[32,4,640]{2,1,0:T(4,128)(2,1)S(1)}, u32[]{:S(2)}, u32[]{:S(2)}) %all-to-all-start.2) | async-done | bytes 163872 | tf_op jit(solution)/shard_map/all_to_all | solution.py:133
  94.6 0.7 gather_fusion.3
  95.4 5.6 %fusion.57 = f32[128,5120]{1,0:T(8,128)} fusion(bf16[128,640]{1,0:T(8,128)(2,1)S(1)} %bitcast.144, bf16[640,5120]{1,0:T(8,128)(2,1)} %param.15), kind=kOutput, calls=%fused_computation.94 | convolution fusion | flops 838860800 | bytes 9338880 | tf_op jit(solution)/shard_map/dot_general | solution.py:136
  101.0 53.4 %all-reduce.1 = bf16[128,5120]{1,0:T(8,128)(2,1)} all-reduce(f32[128,5120]{1,0:T(8,128)} %fusion.57), channel_id=1, replica_groups=mesh['replica'=32,'tensor'=4] {'tensor'}, use_global_device_ids=true, to_apply=%region_9.10 | all-reduce | flops 655360 | bytes 3932160 | tf_op jit(solution)/shard_map/psum | solution.py:137
  (43 shorter events, 1.2 us)
Async XLA Ops:
  0.0 26.5 %copy-start = (bf16[5120,128]{1,0:T(8,128)(2,1)S(1)}, bf16[5120,128]{1,0:T(8,128)(2,1)}, u32[]{:S(2)}) copy-start(bf16[5120,128]{1,0:T(8,128)(2,1)} %param.13) | copy-start | bytes 3932164
  1.6 44.4 %all-to-all-start = ((s32[32,1,2]{2,1,0:T(1,128)}), s32[32,1,2]{2,1,0:T(1,128)S(1)}, u32[]{:S(2)}, u32[]{:S(2)}) async-start(s32[32,1,2]{2,1,0:T(1,128)} %copy.136), calls=%async_computation | async-start | bytes 32768 | tf_op jit(solution)/shard_map/all_to_all | solution.py:95
  11.7 9.7 %copy-start.1 = (bf16[4,32,5120]{2,1,0:T(8,128)(2,1)S(1)}, bf16[4,32,5120]{2,1,0:T(8,128)(2,1)}, u32[]{:S(2)}) copy-start(bf16[4,32,5120]{2,1,0:T(8,128)(2,1)} %param.10) | copy-start | bytes 3932164
  11.7 9.7 %copy-start.8 = (f32[5120]{0:T(1024)S(1)}, f32[5120]{0:T(1024)}, u32[]{:S(2)}) copy-start(f32[5120]{0:T(1024)} %param.11) | copy-start | bytes 61444
  26.5 1.3 copy-start.7
  27.8 0.7 copy-start.5
  49.3 16.0 %all-to-all-start.1 = ((bf16[32,4,7,128]{3,1,2,0:T(4,128)(2,1)}), bf16[32,4,7,128]{3,1,2,0:T(4,128)(2,1)S(1)}, u32[]{:S(2)}, u32[]{:S(2)}) async-start(bf16[32,4,7,128]{3,1,2,0:T(4,128)(2,1)} %gather_fusion.2), calls=%async_computation.1 | async-start | bytes 458752 | tf_op jit(solution)/shard_map/all_to_all | solution.py:105
  65.3 0.7 copy-start.3
  65.4 4.4 %copy-start.2 = (bf16[32,4,5,128]{3,1,2,0:T(4,128)(2,1)}, bf16[32,4,5,128]{3,1,2,0:T(4,128)(2,1)S(1)}, u32[]{:S(2)}) copy-start(bf16[32,4,5,128]{3,1,2,0:T(4,128)(2,1)S(1)} %slice.58) | copy-start | bytes 491524
  75.2 4.8 %copy-start.4 = (f32[32,4,5]{0,1,2:T(4,128)S(1)}, f32[32,4,5]{0,1,2:T(4,128)}, u32[]{:S(2)}) copy-start(f32[32,4,5]{0,1,2:T(4,128)} %copy.145) | copy-start | bytes 7684
  81.3 5.2 %copy-start.6 = (s32[32]{0:T(128)S(1)}, s32[32]{0:T(128)}, u32[]{:S(2)}) copy-start(s32[32]{0:T(128)} %get-tuple-element.5) | copy-start | bytes 388
  82.6 12.0 %all-to-all-start.2 = ((bf16[32,4,640]{2,1,0:T(4,128)(2,1)}), bf16[32,4,640]{2,1,0:T(4,128)(2,1)S(1)}, u32[]{:S(2)}, u32[]{:S(2)}) async-start(bf16[32,4,640]{2,1,0:T(4,128)(2,1)} %copy.155), calls=%async_computation.2 | async-start | bytes 327680 | tf_op jit(solution)/shard_map/all_to_all | solution.py:133

commit v2 on v0

v2 whole, which is shorter than its diff:
```python
import functools
import math

import jax
import jax.numpy as jnp
from jax import lax
from jax.experimental import pallas as pl
from jax.experimental.pallas import tpu as pltpu
from jax.sharding import PartitionSpec as P

HD = 128
MSG = 32
ROPE_BASE = 1000000.0
EPSILON = 1e-06
MESH = pl.DeviceIdType.MESH
F32 = jnp.float32
BF16 = jnp.bfloat16


def mod(value, size):
    return lax.rem(value + 2 * size, size)


def kernel(
    sizes,
    dest_sm, len_sm, table_sm, gain_ref, hid_hbm, wq_hbm, wk_hbm, wv_hbm, wo_hbm, kv_hbm,
    out_hbm,
    hid, wall, kv, wo, acc, code, code_sm, meta_out, meta_in, pick, unpick, stack,
    q_out, q_in, h_out, h_in, heads, part, far, near_r, near_l, got, final,
    hid_sem, w_sem, kv_sem, wo_sem, code_sem,
    meta_send, meta_recv, q_send, q_recv, h_send, h_recv, x_send, x_recv, out_sem,
):
    R, T, S, NQ, D, KC = sizes
    M = S * R
    NH = NQ + 2
    me = lax.axis_index("replica")
    tx = lax.axis_index("tensor")
    chunks = D // KC
    DC = D // T
    half = M // 2
    pages = kv.shape[0]
    max_pages = pages // R
    page = kv.shape[2]

    def weight_copies(c):
        rows = pl.ds(pl.multiple_of(c * KC, KC), KC)
        return (
            pltpu.make_async_copy(wq_hbm.at[rows], wall.at[rows, 0 : NQ * HD], w_sem.at[c, 0]),
            pltpu.make_async_copy(wk_hbm.at[rows], wall.at[rows, NQ * HD : (NQ + 1) * HD], w_sem.at[c, 1]),
            pltpu.make_async_copy(wv_hbm.at[rows], wall.at[rows, (NQ + 1) * HD :], w_sem.at[c, 2]),
        )

    hid_copy = pltpu.make_async_copy(hid_hbm, hid, hid_sem)
    hid_copy.start()
    for c in range(chunks):
        for copy in weight_copies(c):
            copy.start()

    barrier = pltpu.get_barrier_semaphore()

    def greet(k, carry):
        pl.semaphore_signal(barrier, inc=1, device_id={"replica": mod(me + k, R)}, device_id_type=MESH)
        return carry

    lax.fori_loop(1, R, greet, 0)
    right = mod(tx + 1, T)
    left = mod(tx - 1, T)
    for other in (right, left):
        pl.semaphore_signal(barrier, inc=1, device_id={"tensor": other}, device_id_type=MESH)

    numbers = lax.broadcasted_iota(jnp.int32, (R, 128), 0)
    codes = jnp.zeros((R, 128), jnp.int32)
    for b in range(R):
        codes = jnp.where(numbers == dest_sm[b], len_sm[b] * R + b, codes)
    code[...] = codes
    code_copy = pltpu.make_async_copy(code, code_sm, code_sem)
    code_copy.start()
    for n in range(R):
        meta_out[n] = jnp.broadcast_to(codes[n : n + 1], (8, 128))

    pl.semaphore_wait(barrier, R - 1 + 2)

    def send_meta(k, carry):
        n = mod(me + k, R)
        pltpu.make_async_remote_copy(
            src_ref=meta_out.at[n], dst_ref=meta_in.at[me], send_sem=meta_send, recv_sem=meta_recv,
            device_id={"replica": n}, device_id_type=MESH,
        ).start()
        return carry

    lax.fori_loop(1, R, send_meta, 0)

    hid_copy.wait()
    squares = jnp.zeros((M, 128), F32)
    for c in range(D // 128):
        wide = hid[:, c * 128 : (c + 1) * 128].astype(F32)
        squares = squares + wide * wide
    scale = lax.rsqrt(jnp.sum(squares, 1, keepdims=True) * (1.0 / D) + EPSILON)

    acc[...] = jnp.zeros_like(acc)

    def project(c, carry):
        for copy in weight_copies(c):
            copy.wait()
        cols = pl.ds(pl.multiple_of(c * KC, KC), KC)
        normed = (hid[:, cols].astype(F32) * scale * gain_ref[:, cols]).astype(BF16)
        acc[...] += jnp.dot(normed, wall[cols, :], preferred_element_type=F32)
        return carry

    early = chunks // 2
    lax.fori_loop(0, early, project, 0)

    kv_copies = []
    step = pages // 4
    for c in range(4):
        rows = pl.ds(c * step, step)
        kv_copies.append(pltpu.make_async_copy(kv_hbm.at[rows], kv.at[rows], kv_sem.at[c]))
        kv_copies[-1].start()

    meta_all = pltpu.make_async_copy(meta_in.at[pl.ds(0, R - 1)], meta_in.at[pl.ds(0, R - 1)], meta_recv)
    meta_all.wait()
    meta_in[me] = meta_out[me]

    slot_rows = lax.broadcasted_iota(jnp.int32, (R, 128), 0)
    lens = jnp.zeros((R, 128), jnp.int32)
    msg_row = lax.broadcasted_iota(jnp.int32, (MSG, 128), 0)
    lane = lax.broadcasted_iota(jnp.int32, (MSG, 128), 1)
    for o in range(R):
        tile = meta_in[o]
        slot = tile & (R - 1)
        slot_wide = jnp.concatenate([slot] * (R // 8), 0)
        len_wide = jnp.concatenate([lax.shift_right_logical(tile, int(math.log2(R)))] * (R // 8), 0)
        lens = jnp.where(slot_rows == slot_wide, len_wide, lens)
        target = R * msg_row + jnp.concatenate([slot] * (MSG // 8), 0)
        for c in range(0, NH * M, 128):
            width = min(128, NH * M - c)
            hit = jnp.where(target == lane + c, 1.0, 0.0).astype(BF16)
            pick[pl.ds(o * MSG, MSG), c : c + width] = hit[:, :width]
    per = 128 // MSG
    group_of_lane = lax.broadcasted_iota(jnp.int32, (8, 128), 1) // MSG
    row_of_lane = lax.broadcasted_iota(jnp.int32, (8, 128), 1) % MSG
    wide_row = lax.broadcasted_iota(jnp.int32, (NQ * M, 128), 0)
    for g in range(R // per):
        slots = jnp.zeros((8, 128), jnp.int32)
        for i in range(per):
            slots = jnp.where(group_of_lane == i, meta_in[g * per + i] & (R - 1), slots)
        target = jnp.concatenate([R * row_of_lane + slots] * (NQ * M // 8), 0)
        unpick[:, g * 128 : (g + 1) * 128] = jnp.where(target == wide_row, 1.0, 0.0).astype(BF16)

    freq_lane = lax.broadcasted_iota(jnp.int32, (8, 128), 1) % (HD // 2)
    freq = jnp.exp(freq_lane.astype(F32) * (-2.0 / HD * math.log(ROPE_BASE)))
    angle = lens.astype(F32) * jnp.concatenate([freq] * (R // 8), 0)
    cos_len, sin_len = jnp.cos(angle), jnp.sin(angle)
    sign = jnp.where(lax.broadcasted_iota(jnp.int32, (R, 128), 1) < HD // 2, -1.0, 1.0)
    cosines, sines = [], []
    for s in range(S):
        if s == 0:
            cosines.append(cos_len)
            sines.append(sin_len * sign)
            continue
        cos_s = jnp.concatenate([jnp.cos(freq * float(s))] * (R // 8), 0)
        sin_s = jnp.concatenate([jnp.sin(freq * float(s))] * (R // 8), 0)
        cosines.append(cos_len * cos_s - sin_len * sin_s)
        sines.append((sin_len * cos_s + cos_len * sin_s) * sign)
    cosine = jnp.concatenate(cosines, 0)
    sine = jnp.concatenate(sines, 0)

    lax.fori_loop(early, chunks, project, 0)

    wo_copy = pltpu.make_async_copy(wo_hbm, wo, wo_sem)
    wo_copy.start()

    for h in range(NH):
        vec = acc[:, h * HD : (h + 1) * HD]
        if h <= NQ:
            vec = vec * cosine + pltpu.roll(vec, HD // 2, 1) * sine
        stack[h * M : (h + 1) * M, :] = vec.astype(BF16)
    q_out[...] = jnp.dot(pick[...], stack[...], preferred_element_type=F32).astype(BF16).reshape(R, MSG, HD)

    def send_q(k, carry):
        o = mod(me + k, R)
        pltpu.make_async_remote_copy(
            src_ref=q_out.at[o], dst_ref=q_in.at[me], send_sem=q_send, recv_sem=q_recv.at[me],
            device_id={"replica": o}, device_id_type=MESH,
        ).start()
        return carry

    lax.fori_loop(1, R, send_q, 0)
    q_in[me] = q_out[me]

    code_copy.wait()
    for copy in kv_copies:
        copy.wait()

    tok = lax.broadcasted_iota(jnp.int32, (MSG, page), 1)
    f_row = lax.broadcasted_iota(jnp.int32, (MSG, MSG), 0) % S
    f_col = lax.broadcasted_iota(jnp.int32, (MSG, MSG), 1) - NQ * S
    fresh_ok = (f_col >= 0) & (f_col <= f_row)
    factor = 1.0 / math.sqrt(HD)
    dims = (((1,), (1,)), ((), ()))

    def attend(n):
        word = code_sm[n, 0]
        slot = word & (R - 1)
        length = lax.shift_right_logical(word, int(math.log2(R)))
        where = [table_sm[p, slot] for p in range(max_pages)]
        q = q_in[n]
        scores = []
        for p in range(max_pages):
            sc = lax.dot_general(q, kv[where[p], 0], dims, preferred_element_type=F32) * factor
            scores.append(jnp.where(tok < length - p * page, sc, -jnp.inf))
        fresh = lax.dot_general(q, q, dims, preferred_element_type=F32) * factor
        fresh = jnp.where(fresh_ok, fresh, -jnp.inf)
        top = functools.reduce(jnp.maximum, scores)
        peak = jnp.maximum(jnp.max(top, 1, keepdims=True), jnp.max(fresh, 1, keepdims=True))
        w_fresh = jnp.exp(fresh - peak).astype(BF16)
        values = pltpu.roll(q.astype(F32), MSG - S, 0).astype(BF16)
        total = jnp.dot(w_fresh, values, preferred_element_type=F32)
        weight = jnp.zeros((MSG, page), F32)
        for p in range(max_pages):
            w = jnp.exp(scores[p] - peak).astype(BF16)
            weight = weight + w.astype(F32)
            total = total + jnp.dot(w, kv[where[p], 1], preferred_element_type=F32)
        denom = jnp.sum(weight, 1, keepdims=True) + jnp.sum(w_fresh.astype(F32), 1, keepdims=True)
        h_out[n] = (total / denom).astype(BF16)

    def wait_q(n):
        pltpu.make_async_copy(q_in.at[n], q_in.at[n], q_recv.at[n]).wait()

    def send_heads(n):
        pltpu.make_async_remote_copy(
            src_ref=h_out.at[n], dst_ref=h_in.at[me], send_sem=h_send, recv_sem=h_recv,
            device_id={"replica": n}, device_id_type=MESH,
        ).start()

    unroll = 4

    def attend_group(i, carry):
        them = [mod(me - (unroll * i + u + 1), R) for u in range(unroll)]
        for n in them:
            wait_q(n)
        for n in them:
            attend(n)
        for n in them:
            send_heads(n)
        return carry

    lax.fori_loop(0, R // unroll - 1, attend_group, 0)
    last = [mod(me - (R - unroll + u + 1), R) for u in range(unroll - 1)]
    for n in last:
        wait_q(n)
    for n in last:
        attend(n)
    for n in last:
        send_heads(n)
    attend(me)
    h_in[me] = h_out[me]

    wo_copy.wait()
    pltpu.make_async_copy(h_in.at[pl.ds(0, R - 1)], h_in.at[pl.ds(0, R - 1)], h_recv).wait()
    flat = h_in[...].reshape(R * MSG, HD)
    by_head = jnp.dot(unpick[...], flat, preferred_element_type=F32).astype(BF16)
    for h in range(NQ):
        heads[:, h * HD : (h + 1) * HD] = by_head[h * M : (h + 1) * M]

    def cols_of(c):
        return pl.ds(pl.multiple_of(c * DC, DC), DC)

    def partial(c):
        return jnp.dot(heads[...], wo[:, cols_of(c)], preferred_element_type=F32)

    def push(src, dst, i, other):
        copy = pltpu.make_async_remote_copy(
            src_ref=src, dst_ref=dst, send_sem=x_send.at[i], recv_sem=x_recv.at[i],
            device_id={"tensor": other}, device_id_type=MESH,
        )
        copy.start()
        return copy

    low, high = slice(0, half), slice(half, M)
    far[...] = partial(mod(tx + 2, T)).astype(BF16)
    c0 = push(far.at[low], got.at[0], 0, right)
    c1 = push(far.at[high], got.at[1], 1, left)
    sum_r = partial(right)
    near_r[high] = sum_r[half:].astype(BF16)
    c2 = push(near_r.at[high], got.at[2], 2, right)
    sum_l = partial(left)
    near_l[low] = sum_l[:half].astype(BF16)
    c3 = push(near_l.at[low], got.at[3], 3, left)
    part[...] = partial(tx)
    c0.wait_recv()
    near_r[low] = (sum_r[:half] + got[0].astype(F32)).astype(BF16)
    c4 = push(near_r.at[low], got.at[4], 4, right)
    c1.wait_recv()
    near_l[high] = (sum_l[half:] + got[1].astype(F32)).astype(BF16)
    c5 = push(near_l.at[high], got.at[5], 5, left)
    c3.wait_recv()
    c4.wait_recv()
    final[low] = (part[low] + got[3].astype(F32) + got[4].astype(F32)).astype(BF16)
    mine = out_hbm.at[:, cols_of(tx)]
    c6 = push(final.at[low], mine.at[low], 6, right)
    c2.wait_recv()
    c5.wait_recv()
    final[high] = (part[high] + got[2].astype(F32) + got[5].astype(F32)).astype(BF16)
    c7 = push(final.at[high], mine.at[high], 7, left)
    c8 = push(final.at[high], mine.at[high], 8, right)
    c9 = push(final.at[low], mine.at[low], 9, left)
    own = pltpu.make_async_copy(final, mine, out_sem)
    own.start()
    from_left = out_hbm.at[low, cols_of(left)]
    from_right = out_hbm.at[high, cols_of(right)]
    c6.wait_recv()
    c10 = push(from_left, from_left, 10, right)
    c7.wait_recv()
    c11 = push(from_right, from_right, 11, left)
    for copy in (c8, c9, c10, c11):
        copy.wait_recv()
    for copy in (c0, c1, c2, c3, c4, c5, c6, c7, c8, c9, c10, c11):
        copy.wait_send()
    own.wait()
    some = pl.ds(0, R - 1)
    pltpu.make_async_copy(meta_out.at[some], meta_out.at[some], meta_send).wait()
    pltpu.make_async_copy(q_out.at[some], q_out.at[some], q_send).wait()
    pltpu.make_async_copy(h_out.at[some], h_out.at[some], h_send).wait()


def shards(
    replicas, tensors, hidden_in, norm_gain, w_query, w_key, w_value, w_out, kv_pages, lengths, page_table, destination
):
    S, R, D = hidden_in.shape
    T = tensors
    NQ = w_query.shape[1] // HD
    NH = NQ + 2
    M = S * R
    KC = min(512, D // 2)
    DC = D // T
    pages, _, page, _ = kv_pages.shape
    any_spec = pl.BlockSpec(memory_space=pl.ANY)
    smem = pl.BlockSpec(memory_space=pltpu.SMEM)
    dma = pltpu.SemaphoreType.DMA
    out = pl.pallas_call(
        functools.partial(kernel, (R, T, S, NQ, D, KC)),
        out_shape=jax.ShapeDtypeStruct((M, D), BF16),
        in_specs=[smem, smem, smem, pl.BlockSpec(memory_space=pltpu.VMEM)] + [any_spec] * 6,
        out_specs=any_spec,
        scratch_shapes=[
            pltpu.VMEM((M, D), BF16),
            pltpu.VMEM((D, NH * HD), BF16),
            pltpu.VMEM(kv_pages.shape, BF16),
            pltpu.VMEM(w_out.shape, BF16),
            pltpu.VMEM((M, NH * HD), F32),
            pltpu.VMEM((R, 128), jnp.int32),
            pltpu.SMEM((R, 128), jnp.int32),
            pltpu.VMEM((R, 8, 128), jnp.int32),
            pltpu.VMEM((R, 8, 128), jnp.int32),
            pltpu.VMEM((R * MSG, NH * M), BF16),
            pltpu.VMEM((NQ * M, R * MSG), BF16),
            pltpu.VMEM((NH * M, HD), BF16),
            pltpu.VMEM((R, MSG, HD), BF16),
            pltpu.VMEM((R, MSG, HD), BF16),
            pltpu.VMEM((R, MSG, HD), BF16),
            pltpu.VMEM((R, MSG, HD), BF16),
            pltpu.VMEM((M, NQ * HD), BF16),
            pltpu.VMEM((M, DC), F32),
            pltpu.VMEM((M, DC), BF16),
            pltpu.VMEM((M, DC), BF16),
            pltpu.VMEM((M, DC), BF16),
            pltpu.VMEM((6, M // 2, DC), BF16),
            pltpu.VMEM((M, DC), BF16),
            dma, dma((D // KC, 3)), dma((4,)), dma, dma,
            dma, dma, dma, dma((R,)), dma, dma, dma((12,)), dma((12,)), dma,
        ],
        compiler_params=pltpu.CompilerParams(
            collective_id=0, has_side_effects=True, vmem_limit_bytes=58 * 1024 * 1024
        ),
        name="decode_attention",
    )(
        destination, lengths, page_table.T, norm_gain.reshape(1, D), hidden_in.reshape(M, D),
        w_query, w_key, w_value, w_out, kv_pages,
    )
    return out.reshape(S, R, D)


def solution(mesh):
    in_specs = (
        P(None, "replica", None),
        P(),
        P(None, "tensor"),
        P(None, "tensor"),
        P(None, "tensor"),
        P("tensor", None),
        P("replica", None, None, "tensor"),
        P("replica"),
        P("replica", None),
        P("replica"),
    )
    body = functools.partial(shards, mesh.shape["replica"], mesh.shape["tensor"])
    return jax.shard_map(
        body, mesh=mesh, in_specs=in_specs, out_specs=P(None, "replica", None), check_vma=False
    )
```

time: 235 us -> 66.3 us (0.28)
  the two profiles are of different devices: /device:TPU:32 before, /device:TPU:0 now
where the time goes in v2:
time: 66.3 us; the launch traced here: 66.1 us
  Pallas kernels  63.7 us (96%)
  local copies, waits for them, and re-layouts  2.46 us (4%)
    pallas_call x1, Pallas kernels, shards(): pl.pallas_call(functools.partial(kernel, (R, T, S, NQ, D, KC)), out_shape...  63.7 us
    unnamed x1, local copies, waits for them, and re-layouts  2.46 us

profile of v2, /device:TPU:0, one launch (start us, length us, event | category | flops | bytes accessed | tf_op | source)
XLA Modules:
  0.0 66.1 jit_solution(14028122036396673998)
XLA Ops:
  0.0 63.7 %decode_attention.1 = bf16[128,5120]{1,0:T(8,128)(2,1)} custom-call(s32[32]{0:T(128)} %dest_sm.1, s32[32]{0:T(128)} %len_sm.1, s32[4,32]{1,0:T(4,128)} %bitcast.7, f32[1,5120]{1,0:T(1,128)} %bitcast.6, bf16[128,5120]{1,0:T(8,128)(2,1)} %bitcast.5, bf16[5120,640]{1,0:T(8,128)(2,1)} %wq_hbm.1, bf16[5120,128]{1,0:T(8,128)(2,1)} %wk_hbm.1, ...), custom_call_target="tpu_custom_call" | custom-call | tf_op jit(solution)/shard_map/decode_attention/pallas_call | solution.py:341
  63.7 2.5 %copy.12 = bf16[4,32,5120]{2,1,0:T(8,128)(2,1)} copy(bf16[4,32,5120]{2,1,0:T(8,128)(2,1)} %bitcast.4) | data formatting | bytes 2621440

commit v3 on v2

v3 whole, which is shorter than its diff:
```python
import functools
import math

import jax
import jax.numpy as jnp
from jax import lax
from jax.experimental import pallas as pl
from jax.experimental.pallas import tpu as pltpu
from jax.sharding import PartitionSpec as P

HD = 128
GROUP = 4
MSG = 32
ROPE_BASE = 1000000.0
EPSILON = 1e-06
SUBS = 2
MESH = pl.DeviceIdType.MESH
F32 = jnp.float32
BF16 = jnp.bfloat16


def mod(value, size):
    return lax.rem(value + 2 * size, size)


def settle(ref, sem):
    pltpu.make_async_copy(ref, ref, sem).wait()


def kernel(
    sizes,
    dest_sm, len_sm, table_sm, gain_ref, hid_hbm, wq_hbm, wk_hbm, wv_hbm, wo_hbm, kv_hbm,
    out_hbm,
    hid, wall, kv, wo, acc, code, code_sm, meta_out, meta_in, pick, unpick, stack,
    q_out, q_in, h_out, h_in, heads, part, sums_r, sums_l, far, near_r, near_l, got, final,
    hid_sem, w_sem, kv_sem, wo_sem, code_sem,
    meta_send, meta_recv, q_send, q_recv, h_send, h_recv, x_send, x_recv, out_sem,
):
    R, T, S, NQ, D, KC = sizes
    M = S * R
    NH = NQ + 2
    me = lax.axis_index("replica")
    tx = lax.axis_index("tensor")
    chunks = D // KC
    group = me // GROUP
    groups = R // GROUP
    DC = D // T
    half = M // 2
    pages = kv.shape[0]
    max_pages = pages // R
    page = kv.shape[2]

    def weight_copies(c):
        rows = pl.ds(pl.multiple_of(c * KC, KC), KC)
        return (
            pltpu.make_async_copy(wq_hbm.at[rows], wall.at[rows, 0 : NQ * HD], w_sem.at[c, 0]),
            pltpu.make_async_copy(wk_hbm.at[rows], wall.at[rows, NQ * HD : (NQ + 1) * HD], w_sem.at[c, 1]),
            pltpu.make_async_copy(wv_hbm.at[rows], wall.at[rows, (NQ + 1) * HD :], w_sem.at[c, 2]),
        )

    hid_copy = pltpu.make_async_copy(hid_hbm, hid, hid_sem)
    hid_copy.start()
    ahead = 2
    for c in range(ahead):
        for copy in weight_copies(c):
            copy.start()

    barrier = pltpu.get_barrier_semaphore()

    def greet(k, carry):
        pl.semaphore_signal(barrier, inc=1, device_id={"replica": mod(me + k, R)}, device_id_type=MESH)
        return carry

    lax.fori_loop(1, R, greet, 0)
    right = mod(tx + 1, T)
    left = mod(tx - 1, T)
    for other in (right, left):
        pl.semaphore_signal(barrier, inc=1, device_id={"tensor": other}, device_id_type=MESH)

    numbers = lax.broadcasted_iota(jnp.int32, (R, 128), 0)
    codes = jnp.zeros((R, 128), jnp.int32)
    for b in range(R):
        codes = jnp.where(numbers == dest_sm[b], len_sm[b] * R + b, codes)
    code[...] = codes
    code_copy = pltpu.make_async_copy(code, code_sm, code_sem)
    code_copy.start()
    for n in range(R):
        meta_out[n] = jnp.broadcast_to(codes[n : n + 1], (8, 128))

    pl.semaphore_wait(barrier, R - 1 + 2)

    def to_all(make):
        def send(k, carry):
            n = mod(group * GROUP + GROUP + k, R)

            @pl.when(n != me)
            def _():
                make(n).start()

            return carry

        lax.fori_loop(0, R, send, 0)

    def meta_copy(n):
        return pltpu.make_async_remote_copy(
            src_ref=meta_out.at[n], dst_ref=meta_in.at[me], send_sem=meta_send, recv_sem=meta_recv,
            device_id={"replica": n}, device_id_type=MESH,
        )

    to_all(meta_copy)

    hid_copy.wait()
    squares = jnp.zeros((M, 128), F32)
    for c in range(D // 128):
        wide = hid[:, c * 128 : (c + 1) * 128].astype(F32)
        squares = squares + wide * wide
    scale = lax.rsqrt(jnp.sum(squares, 1, keepdims=True) * (1.0 / D) + EPSILON)

    for c in range(0, D, 512):
        cols = slice(c, c + 512)
        hid[:, cols] = (hid[:, cols].astype(F32) * scale * gain_ref[:, cols]).astype(BF16)

    kv_copies = []
    step = pages // 4
    for c in range(4):
        rows = pl.ds(c * step, step)
        kv_copies.append(pltpu.make_async_copy(kv_hbm.at[rows], kv.at[rows], kv_sem.at[c]))

    def project(c):
        for copy in weight_copies(c):
            copy.wait()
        if c + ahead < chunks:
            for copy in weight_copies(c + ahead):
                copy.start()
        elif c + ahead == chunks:
            kv_copies[0].start()
            kv_copies[1].start()
        cols = slice(c * KC, (c + 1) * KC)
        term = jnp.dot(hid[:, cols], wall[cols, :], preferred_element_type=F32)
        acc[...] = term if c == 0 else acc[...] + term

    early = chunks // 2
    for c in range(early):
        project(c)

    settle(meta_in.at[pl.ds(0, R - 1)], meta_recv)
    meta_in[me] = meta_out[me]

    slot_rows = lax.broadcasted_iota(jnp.int32, (R, 128), 0)
    lens = jnp.zeros((R, 128), jnp.int32)
    msg_row = lax.broadcasted_iota(jnp.int32, (MSG, 128), 0)
    lane = lax.broadcasted_iota(jnp.int32, (MSG, 128), 1)
    for o in range(R):
        tile = meta_in[o]
        slot = tile & (R - 1)
        slot_wide = jnp.concatenate([slot] * (R // 8), 0)
        len_wide = jnp.concatenate([lax.shift_right_logical(tile, int(math.log2(R)))] * (R // 8), 0)
        lens = jnp.where(slot_rows == slot_wide, len_wide, lens)
        target = R * msg_row + jnp.concatenate([slot] * (MSG // 8), 0)
        for c in range(0, NH * M, 128):
            width = min(128, NH * M - c)
            hit = jnp.where(target == lane + c, 1.0, 0.0).astype(BF16)
            pick[pl.ds(o * MSG, MSG), c : c + width] = hit[:, :width]
    freq_lane = lax.broadcasted_iota(jnp.int32, (8, 128), 1) % (HD // 2)
    freq = jnp.exp(freq_lane.astype(F32) * (-2.0 / HD * math.log(ROPE_BASE)))
    angle = lens.astype(F32) * jnp.concatenate([freq] * (R // 8), 0)
    cos_len, sin_len = jnp.cos(angle), jnp.sin(angle)
    sign = jnp.where(lax.broadcasted_iota(jnp.int32, (R, 128), 1) < HD // 2, -1.0, 1.0)
    cosines, sines = [], []
    for s in range(S):
        if s == 0:
            cosines.append(cos_len)
            sines.append(sin_len * sign)
            continue
        cos_s = jnp.concatenate([jnp.cos(freq * float(s))] * (R // 8), 0)
        sin_s = jnp.concatenate([jnp.sin(freq * float(s))] * (R // 8), 0)
        cosines.append(cos_len * cos_s - sin_len * sin_s)
        sines.append((sin_len * cos_s + cos_len * sin_s) * sign)
    cosine = jnp.concatenate(cosines, 0)
    sine = jnp.concatenate(sines, 0)

    for c in range(early, chunks):
        project(c)
    kv_copies[2].start()
    kv_copies[3].start()

    for h in range(NH):
        vec = acc[:, h * HD : (h + 1) * HD]
        if h <= NQ:
            vec = vec * cosine + pltpu.roll(vec, HD // 2, 1) * sine
        stack[h * M : (h + 1) * M, :] = vec.astype(BF16)
    q_out[...] = jnp.dot(pick[...], stack[...], preferred_element_type=F32).astype(BF16).reshape(R, MSG, HD)

    def q_copy(o):
        return pltpu.make_async_remote_copy(
            src_ref=q_out.at[o], dst_ref=q_in.at[me], send_sem=q_send, recv_sem=q_recv.at[me],
            device_id={"replica": o}, device_id_type=MESH,
        )

    to_all(q_copy)
    q_in[me] = q_out[me]
    wo_copy = pltpu.make_async_copy(wo_hbm, wo, wo_sem)
    wo_copy.start()

    per = 128 // MSG
    group_of_lane = lax.broadcasted_iota(jnp.int32, (8, 128), 1) // MSG
    row_of_lane = lax.broadcasted_iota(jnp.int32, (8, 128), 1) % MSG
    wide_row = lax.broadcasted_iota(jnp.int32, (NQ * M, 128), 0)
    for g in range(R // per):
        slots = jnp.zeros((8, 128), jnp.int32)
        for i in range(per):
            slots = jnp.where(group_of_lane == i, meta_in[g * per + i] & (R - 1), slots)
        target = jnp.concatenate([R * row_of_lane + slots] * (NQ * M // 8), 0)
        unpick[:, g * 128 : (g + 1) * 128] = jnp.where(target == wide_row, 1.0, 0.0).astype(BF16)

    code_copy.wait()
    for copy in kv_copies:
        copy.wait()

    span = max_pages * page
    rows = GROUP * MSG
    tok = lax.broadcasted_iota(jnp.int32, (MSG, span), 1)
    f_row = lax.broadcasted_iota(jnp.int32, (rows, rows), 0)
    f_col = lax.broadcasted_iota(jnp.int32, (rows, rows), 1)
    f_key = f_col % MSG - NQ * S
    fresh_ok = (f_row // MSG == f_col // MSG) & (f_key >= 0) & (f_key <= f_row % S)
    factor = math.log2(math.e) / math.sqrt(HD)
    dims = (((1,), (1,)), ((), ()))

    def attend(g):
        first = g * GROUP
        q = q_in[pl.ds(first, GROUP)].reshape(rows, HD)
        fresh = lax.dot_general(q, q, dims, preferred_element_type=F32)
        fresh = jnp.where(fresh_ok, fresh, -jnp.inf)
        places, scores = [], []
        for u in range(GROUP):
            word = code_sm[first + u, 0]
            slot = word & (R - 1)
            length = lax.shift_right_logical(word, int(math.log2(R)))
            places.append([table_sm[p, slot] for p in range(max_pages)])
            keys = jnp.concatenate([kv[at, 0] for at in places[u]], 0)
            sc = lax.dot_general(q[u * MSG : (u + 1) * MSG], keys, dims, preferred_element_type=F32)
            scores.append(jnp.where(tok < length, sc, -jnp.inf))
        values = pltpu.roll(q.astype(F32), rows - S, 0).astype(BF16)
        for u in range(GROUP):
            mine = slice(u * MSG, (u + 1) * MSG)
            peak = jnp.maximum(
                jnp.max(scores[u], 1, keepdims=True), jnp.max(fresh[mine], 1, keepdims=True)
            )
            w_fresh = jnp.exp2((fresh[mine] - peak) * factor).astype(BF16)
            w = jnp.exp2((scores[u] - peak) * factor).astype(BF16)
            total = jnp.dot(w_fresh, values, preferred_element_type=F32)
            cached = jnp.concatenate([kv[at, 1] for at in places[u]], 0)
            total = total + jnp.dot(w, cached, preferred_element_type=F32)
            denom = jnp.sum(w.astype(F32), 1, keepdims=True) + jnp.sum(
                w_fresh.astype(F32), 1, keepdims=True
            )
            h_out[first + u] = (total / denom).astype(BF16)

    def wait_q(n):
        settle(q_in.at[n], q_recv.at[n])

    def heads_copy(n):
        return pltpu.make_async_remote_copy(
            src_ref=h_out.at[n], dst_ref=h_in.at[me], send_sem=h_send, recv_sem=h_recv,
            device_id={"replica": n}, device_id_type=MESH,
        )

    def attend_group(i, carry):
        g = mod(group - 1 - i, groups)
        for u in range(GROUP):
            n = g * GROUP + u

            @pl.when(n != me)
            def _():
                wait_q(n)

        attend(g)
        for u in range(GROUP):
            n = g * GROUP + u

            @pl.when(n != me)
            def _():
                heads_copy(n).start()

        return carry

    lax.fori_loop(0, groups, attend_group, 0)
    h_in[me] = h_out[me]

    wo_copy.wait()
    settle(h_in.at[pl.ds(0, R - 1)], h_recv)
    flat = h_in[...].reshape(R * MSG, HD)
    by_head = jnp.dot(unpick[...], flat, preferred_element_type=F32).astype(BF16)
    for h in range(NQ):
        heads[:, h * HD : (h + 1) * HD] = by_head[h * M : (h + 1) * M]

    wide = DC // SUBS

    def cols_of(c, b):
        return pl.ds(pl.multiple_of(c * DC + b * wide, 128), wide)

    def partial(c, b):
        return jnp.dot(heads[...], wo[:, cols_of(c, b)], preferred_element_type=F32)

    copies = []

    def push(src, dst, b, i, other):
        copy = pltpu.make_async_remote_copy(
            src_ref=src, dst_ref=dst, send_sem=x_send.at[b, i], recv_sem=x_recv.at[b, i],
            device_id={"tensor": other}, device_id_type=MESH,
        )
        copy.start()
        copies.append(copy)
        return copy

    low, high = slice(0, half), slice(half, M)
    subs = range(SUBS)
    c0, c1, c2, c3, c4, c5, c6, c7, c8, c9 = ([] for _ in range(10))
    for b in subs:
        far[b] = partial(mod(tx + 2, T), b).astype(BF16)
        c0.append(push(far.at[b, low], got.at[b, 0], b, 0, right))
        c1.append(push(far.at[b, high], got.at[b, 1], b, 1, left))
    for b in subs:
        sums_r[b] = partial(right, b)
        near_r[b, high] = sums_r[b, high].astype(BF16)
        c2.append(push(near_r.at[b, high], got.at[b, 2], b, 2, right))
        sums_l[b] = partial(left, b)
        near_l[b, low] = sums_l[b, low].astype(BF16)
        c3.append(push(near_l.at[b, low], got.at[b, 3], b, 3, left))
    for b in subs:
        part[b] = partial(tx, b)
    for b in subs:
        c0[b].wait_recv()
        near_r[b, low] = (sums_r[b, low] + got[b, 0].astype(F32)).astype(BF16)
        c4.append(push(near_r.at[b, low], got.at[b, 4], b, 4, right))
        c1[b].wait_recv()
        near_l[b, high] = (sums_l[b, high] + got[b, 1].astype(F32)).astype(BF16)
        c5.append(push(near_l.at[b, high], got.at[b, 5], b, 5, left))
    own = []
    for b in subs:
        mine = out_hbm.at[:, cols_of(tx, b)]
        c3[b].wait_recv()
        c4[b].wait_recv()
        final[b, low] = (part[b, low] + got[b, 3].astype(F32) + got[b, 4].astype(F32)).astype(BF16)
        c6.append(push(final.at[b, low], mine.at[low], b, 6, right))
        c2[b].wait_recv()
        c5[b].wait_recv()
        final[b, high] = (part[b, high] + got[b, 2].astype(F32) + got[b, 5].astype(F32)).astype(BF16)
        c7.append(push(final.at[b, high], mine.at[high], b, 7, left))
        c8.append(push(final.at[b, high], mine.at[high], b, 8, right))
        c9.append(push(final.at[b, low], mine.at[low], b, 9, left))
        own.append(pltpu.make_async_copy(final.at[b], mine, out_sem.at[b]))
        own[b].start()
    last = []
    for b in subs:
        from_left = out_hbm.at[low, cols_of(left, b)]
        from_right = out_hbm.at[high, cols_of(right, b)]
        c6[b].wait_recv()
        last.append(push(from_left, from_left, b, 10, right))
        c7[b].wait_recv()
        last.append(push(from_right, from_right, b, 11, left))
    for copy in c8 + c9 + last:
        copy.wait_recv()
    for copy in copies:
        copy.wait_send()
    for copy in own:
        copy.wait()
    some = pl.ds(0, R - 1)
    settle(meta_out.at[some], meta_send)
    settle(q_out.at[some], q_send)
    settle(h_out.at[some], h_send)


def shards(
    replicas, tensors, hidden_in, norm_gain, w_query, w_key, w_value, w_out, kv_pages, lengths, page_table, destination
):
    S, R, D = hidden_in.shape
    T = tensors
    NQ = w_query.shape[1] // HD
    NH = NQ + 2
    M = S * R
    KC = min(1024, D // 2)
    DC = D // T
    pages, _, page, _ = kv_pages.shape
    any_spec = pl.BlockSpec(memory_space=pl.ANY)
    smem = pl.BlockSpec(memory_space=pltpu.SMEM)
    dma = pltpu.SemaphoreType.DMA
    out = pl.pallas_call(
        functools.partial(kernel, (R, T, S, NQ, D, KC)),
        out_shape=jax.ShapeDtypeStruct((M, D), BF16),
        in_specs=[smem, smem, smem, pl.BlockSpec(memory_space=pltpu.VMEM)] + [any_spec] * 6,
        out_specs=any_spec,
        scratch_shapes=[
            pltpu.VMEM((M, D), BF16),
            pltpu.VMEM((D, NH * HD), BF16),
            pltpu.VMEM(kv_pages.shape, BF16),
            pltpu.VMEM(w_out.shape, BF16),
            pltpu.VMEM((M, NH * HD), F32),
            pltpu.VMEM((R, 128), jnp.int32),
            pltpu.SMEM((R, 128), jnp.int32),
            pltpu.VMEM((R, 8, 128), jnp.int32),
            pltpu.VMEM((R, 8, 128), jnp.int32),
            pltpu.VMEM((R * MSG, NH * M), BF16),
            pltpu.VMEM((NQ * M, R * MSG), BF16),
            pltpu.VMEM((NH * M, HD), BF16),
            pltpu.VMEM((R, MSG, HD), BF16),
            pltpu.VMEM((R, MSG, HD), BF16),
            pltpu.VMEM((R, MSG, HD), BF16),
            pltpu.VMEM((R, MSG, HD), BF16),
            pltpu.VMEM((M, NQ * HD), BF16),
            pltpu.VMEM((SUBS, M, DC // SUBS), F32),
            pltpu.VMEM((SUBS, M, DC // SUBS), F32),
            pltpu.VMEM((SUBS, M, DC // SUBS), F32),
            pltpu.VMEM((SUBS, M, DC // SUBS), BF16),
            pltpu.VMEM((SUBS, M, DC // SUBS), BF16),
            pltpu.VMEM((SUBS, M, DC // SUBS), BF16),
            pltpu.VMEM((SUBS, 6, M // 2, DC // SUBS), BF16),
            pltpu.VMEM((SUBS, M, DC // SUBS), BF16),
            dma, dma((D // KC, 3)), dma((4,)), dma, dma,
            dma, dma, dma, dma((R,)), dma, dma, dma((SUBS, 12)), dma((SUBS, 12)), dma((SUBS,)),
        ],
        compiler_params=pltpu.CompilerParams(
            collective_id=0, has_side_effects=True, vmem_limit_bytes=58 * 1024 * 1024
        ),
        name="decode_attention",
    )(
        destination, lengths, page_table.T, norm_gain.reshape(1, D), hidden_in.reshape(M, D),
        w_query, w_key, w_value, w_out, kv_pages,
    )
    return out.reshape(S, R, D)


def solution(mesh):
    in_specs = (
        P(None, "replica", None),
        P(),
        P(None, "tensor"),
        P(None, "tensor"),
        P(None, "tensor"),
        P("tensor", None),
        P("replica", None, None, "tensor"),
        P("replica"),
        P("replica", None),
        P("replica"),
    )
    body = functools.partial(shards, mesh.shape["replica"], mesh.shape["tensor"])
    return jax.shard_map(
        body, mesh=mesh, in_specs=in_specs, out_specs=P(None, "replica", None), check_vma=False
    )
```

time: 66.3 us -> 58.7 us (0.89)
  Pallas kernels: 63.7 us -> 56.1 us
    pallas_call x1, Pallas kernels: 63.7 us -> 56.1 us  [shards(): pl.pallas_call(functools.partial(kernel, (R, T, S, NQ, D, KC)), out_shape...]
where the time goes in v3:
time: 58.7 us; the launch traced here: 58.5 us
  Pallas kernels  56.1 us (96%)
  local copies, waits for them, and re-layouts  2.46 us (4%)
    pallas_call x1, Pallas kernels, shards(): pl.pallas_call(functools.partial(kernel, (R, T, S, NQ, D, KC)), out_shape...  56.1 us
    unnamed x1, local copies, waits for them, and re-layouts  2.46 us

profile of v3, /device:TPU:0, one launch (start us, length us, event | category | flops | bytes accessed | tf_op | source)
XLA Modules:
  0.0 58.5 jit_solution(12600116129552358541)
XLA Ops:
  0.0 56.1 %decode_attention.1 = bf16[128,5120]{1,0:T(8,128)(2,1)} custom-call(s32[32]{0:T(128)} %dest_sm.1, s32[32]{0:T(128)} %len_sm.1, s32[4,32]{1,0:T(4,128)} %bitcast.7, f32[1,5120]{1,0:T(1,128)} %bitcast.6, bf16[128,5120]{1,0:T(8,128)(2,1)} %bitcast.5, bf16[5120,640]{1,0:T(8,128)(2,1)} %wq_hbm.1, bf16[5120,128]{1,0:T(8,128)(2,1)} %wk_hbm.1, ...), custom_call_target="tpu_custom_call" | custom-call | tf_op jit(solution)/shard_map/decode_attention/pallas_call | solution.py:389
  56.1 2.5 %copy.12 = bf16[4,32,5120]{2,1,0:T(8,128)(2,1)} copy(bf16[4,32,5120]{2,1,0:T(8,128)(2,1)} %bitcast.4) | data formatting | bytes 2621440

commit v4 on v3

--- a/solution.py
+++ b/solution.py
@@ -31,7 +31,7 @@
     sizes,
     dest_sm, len_sm, table_sm, gain_ref, hid_hbm, wq_hbm, wk_hbm, wv_hbm, wo_hbm, kv_hbm,
     out_hbm,
-    hid, wall, kv, wo, acc, code, code_sm, meta_out, meta_in, pick, unpick, stack,
+    hid, wq, wk, wv, kv, wo, acc, code, code_sm, meta_out, meta_in, pick, unpick, stack,
     q_out, q_in, h_out, h_in, heads, part, sums_r, sums_l, far, near_r, near_l, got, final,
     hid_sem, w_sem, kv_sem, wo_sem, code_sem,
     meta_send, meta_recv, q_send, q_recv, h_send, h_recv, x_send, x_recv, out_sem,
@@ -53,17 +53,20 @@
     def weight_copies(c):
         rows = pl.ds(pl.multiple_of(c * KC, KC), KC)
         return (
-            pltpu.make_async_copy(wq_hbm.at[rows], wall.at[rows, 0 : NQ * HD], w_sem.at[c, 0]),
-            pltpu.make_async_copy(wk_hbm.at[rows], wall.at[rows, NQ * HD : (NQ + 1) * HD], w_sem.at[c, 1]),
-            pltpu.make_async_copy(wv_hbm.at[rows], wall.at[rows, (NQ + 1) * HD :], w_sem.at[c, 2]),
+            pltpu.make_async_copy(wq_hbm.at[rows], wq.at[rows], w_sem.at[c, 0]),
+            pltpu.make_async_copy(wk_hbm.at[rows], wk.at[rows], w_sem.at[c, 1]),
+            pltpu.make_async_copy(wv_hbm.at[rows], wv.at[rows], w_sem.at[c, 2]),
         )
 
     hid_copy = pltpu.make_async_copy(hid_hbm, hid, hid_sem)
     hid_copy.start()
-    ahead = 2
-    for c in range(ahead):
-        for copy in weight_copies(c):
-            copy.start()
+    def load(c):
+        if c < chunks:
+            for copy in weight_copies(c):
+                copy.start()
+
+    load(0)
+    load(1)
 
     barrier = pltpu.get_barrier_semaphore()
 
@@ -110,16 +113,20 @@
     to_all(meta_copy)
 
     hid_copy.wait()
+    load(2)
     squares = jnp.zeros((M, 128), F32)
     for c in range(D // 128):
         wide = hid[:, c * 128 : (c + 1) * 128].astype(F32)
         squares = squares + wide * wide
+    load(3)
     scale = lax.rsqrt(jnp.sum(squares, 1, keepdims=True) * (1.0 / D) + EPSILON)
 
     for c in range(0, D, 512):
         cols = slice(c, c + 512)
         hid[:, cols] = (hid[:, cols].astype(F32) * scale * gain_ref[:, cols]).astype(BF16)
 
+    for c in range(4, chunks):
+        load(c)
     kv_copies = []
     step = pages // 4
     for c in range(4):
@@ -129,14 +136,12 @@
     def project(c):
         for copy in weight_copies(c):
             copy.wait()
-        if c + ahead < chunks:
-            for copy in weight_copies(c + ahead):
+        if c + 1 == chunks:
+            for copy in kv_copies:
                 copy.start()
-        elif c + ahead == chunks:
-            kv_copies[0].start()
-            kv_copies[1].start()
         cols = slice(c * KC, (c + 1) * KC)
-        term = jnp.dot(hid[:, cols], wall[cols, :], preferred_element_type=F32)
+        weights = jnp.concatenate([wq[cols], wk[cols], wv[cols]], 1)
+        term = jnp.dot(hid[:, cols], weights, preferred_element_type=F32)
         acc[...] = term if c == 0 else acc[...] + term
 
     early = chunks // 2
@@ -181,8 +186,6 @@
 
     for c in range(early, chunks):
         project(c)
-    kv_copies[2].start()
-    kv_copies[3].start()
 
     for h in range(NH):
         vec = acc[:, h * HD : (h + 1) * HD]
@@ -285,7 +288,7 @@
 
         return carry
 
-    lax.fori_loop(0, groups, attend_group, 0)
+    lax.fori_loop(0, groups, attend_group, 0, unroll=2)
     h_in[me] = h_out[me]
 
     wo_copy.wait()
@@ -303,15 +306,12 @@
     def partial(c, b):
         return jnp.dot(heads[...], wo[:, cols_of(c, b)], preferred_element_type=F32)
 
-    copies = []
-
     def push(src, dst, b, i, other):
         copy = pltpu.make_async_remote_copy(
             src_ref=src, dst_ref=dst, send_sem=x_send.at[b, i], recv_sem=x_recv.at[b, i],
             device_id={"tensor": other}, device_id_type=MESH,
         )
         copy.start()
-        copies.append(copy)
         return copy
 
     low, high = slice(0, half), slice(half, M)
@@ -324,18 +324,23 @@
     for b in subs:
         sums_r[b] = partial(right, b)
         near_r[b, high] = sums_r[b, high].astype(BF16)
-        c2.append(push(near_r.at[b, high], got.at[b, 2], b, 2, right))
         sums_l[b] = partial(left, b)
         near_l[b, low] = sums_l[b, low].astype(BF16)
+    for b in subs:
+        part[b] = partial(tx, b)
+    for b in subs:
+        c0[b].wait_send()
+        c2.append(push(near_r.at[b, high], got.at[b, 2], b, 2, right))
+        c1[b].wait_send()
         c3.append(push(near_l.at[b, low], got.at[b, 3], b, 3, left))
-    for b in subs:
-        part[b] = partial(tx, b)
     for b in subs:
         c0[b].wait_recv()
         near_r[b, low] = (sums_r[b, low] + got[b, 0].astype(F32)).astype(BF16)
+        c2[b].wait_send()
         c4.append(push(near_r.at[b, low], got.at[b, 4], b, 4, right))
         c1[b].wait_recv()
         near_l[b, high] = (sums_l[b, high] + got[b, 1].astype(F32)).astype(BF16)
+        c3[b].wait_send()
         c5.append(push(near_l.at[b, high], got.at[b, 5], b, 5, left))
     own = []
     for b in subs:
@@ -362,7 +367,7 @@
         last.append(push(from_right, from_right, b, 11, left))
     for copy in c8 + c9 + last:
         copy.wait_recv()
-    for copy in copies:
+    for copy in c4 + c5 + c6 + c7 + c8 + c9 + last:
         copy.wait_send()
     for copy in own:
         copy.wait()
@@ -393,7 +398,9 @@
         out_specs=any_spec,
         scratch_shapes=[
             pltpu.VMEM((M, D), BF16),
-            pltpu.VMEM((D, NH * HD), BF16),
+            pltpu.VMEM((D, NQ * HD), BF16),
+            pltpu.VMEM((D, HD), BF16),
+            pltpu.VMEM((D, HD), BF16),
             pltpu.VMEM(kv_pages.shape, BF16),
             pltpu.VMEM(w_out.shape, BF16),
             pltpu.VMEM((M, NH * HD), F32),

time: 58.7 us -> 58.1 us (0.990)
  Pallas kernels: 56.1 us -> 55.4 us
    pallas_call x1, Pallas kernels: 56.1 us -> 55.4 us  [shards(): pl.pallas_call(functools.partial(kernel, (R, T, S, NQ, D, KC)), out_shape...]
where the time goes in v4:
time: 58.1 us; the launch traced here: 57.9 us
  Pallas kernels  55.4 us (95%)
  local copies, waits for them, and re-layouts  2.46 us (4%)
    pallas_call x1, Pallas kernels, shards(): pl.pallas_call(functools.partial(kernel, (R, T, S, NQ, D, KC)), out_shape...  55.4 us
    unnamed x1, local copies, waits for them, and re-layouts  2.46 us

profile of v4, /device:TPU:0, one launch (start us, length us, event | category | flops | bytes accessed | tf_op | source)
XLA Modules:
  0.0 57.9 jit_solution(11511879563677079526)
XLA Ops:
  0.0 55.4 %decode_attention.1 = bf16[128,5120]{1,0:T(8,128)(2,1)} custom-call(s32[32]{0:T(128)} %dest_sm.1, s32[32]{0:T(128)} %len_sm.1, s32[4,32]{1,0:T(4,128)} %bitcast.7, f32[1,5120]{1,0:T(1,128)} %bitcast.6, bf16[128,5120]{1,0:T(8,128)(2,1)} %bitcast.5, bf16[5120,640]{1,0:T(8,128)(2,1)} %wq_hbm.1, bf16[5120,128]{1,0:T(8,128)(2,1)} %wk_hbm.1, ...), custom_call_target="tpu_custom_call" | custom-call | tf_op jit(solution)/shard_map/decode_attention/pallas_call | solution.py:394
  55.4 2.5 %copy.12 = bf16[4,32,5120]{2,1,0:T(8,128)(2,1)} copy(bf16[4,32,5120]{2,1,0:T(8,128)(2,1)} %bitcast.4) | data formatting | bytes 2621440

commit v5 on v4

--- a/solution.py
+++ b/solution.py
@@ -14,6 +14,7 @@
 ROPE_BASE = 1000000.0
 EPSILON = 1e-06
 SUBS = 2
+CHIPS_Z = 4
 MESH = pl.DeviceIdType.MESH
 F32 = jnp.float32
 BF16 = jnp.bfloat16
@@ -30,11 +31,11 @@
 def kernel(
     sizes,
     dest_sm, len_sm, table_sm, gain_ref, hid_hbm, wq_hbm, wk_hbm, wv_hbm, wo_hbm, kv_hbm,
-    out_hbm,
-    hid, wq, wk, wv, kv, wo, acc, code, code_sm, meta_out, meta_in, pick, unpick, stack,
-    q_out, q_in, h_out, h_in, heads, part, sums_r, sums_l, far, near_r, near_l, got, final,
+    out_ref,
+    hid, wq, wk, wv, kv, wf, relay, acc, code, code_sm, meta_out, meta_in, pick, unpick, stack,
+    q_out, q_in, h_out, h_in, heads, total,
     hid_sem, w_sem, kv_sem, wo_sem, code_sem,
-    meta_send, meta_recv, q_send, q_recv, h_send, h_recv, x_send, x_recv, out_sem,
+    meta_send, meta_recv, q_send, q_recv, h_send, h_recv, x_send, x_recv, f_send, f_recv,
 ):
     R, T, S, NQ, D, KC = sizes
     M = S * R
@@ -49,6 +50,60 @@
     pages = kv.shape[0]
     max_pages = pages // R
     page = kv.shape[2]
+    KR = wo_hbm.shape[0]
+    HB, QB = KR // 2, KR // 8
+    HC = DC // 2
+    core = me % 2
+    mate = me + 1 - 2 * core
+    chip = me // 2
+    z, y = chip % CHIPS_Z, chip // CHIPS_Z
+    chips_y = R // (2 * CHIPS_Z)
+    parity = (y + z) % 2
+    opposite = mod(tx + 2, T)
+
+    def at(yy, zz):
+        return (mod(yy, chips_y) * CHIPS_Z + mod(zz, CHIPS_Z)) * 2 + core
+
+    around = (at(y + 1, z), at(y - 1, z), at(y, z + 1), at(y, z - 1))
+
+    def rows_at(owner, first, size):
+        return pl.ds(pl.multiple_of(owner * KR + first, 16), size)
+
+    half_cols = pl.ds(pl.multiple_of(core * HC, 128), HC)
+
+    def own_rows(target, first, size):
+        cols = pl.ds(pl.multiple_of(target * DC + core * HC, 128), HC)
+        return wo_hbm.at[pl.ds(pl.multiple_of(first, 16), size), cols]
+
+    def weight_piece(src, dst, i, other):
+        return pltpu.make_async_remote_copy(
+            src_ref=src, dst_ref=dst, send_sem=f_send.at[i], recv_sem=f_recv.at[i],
+            device_id=other, device_id_type=MESH,
+        )
+
+    def held(owner, first, size):
+        return wf.at[rows_at(owner, first, size), half_cols]
+
+    def same_place(owner, first, size, i, other):
+        return weight_piece(held(owner, first, size), held(owner, first, size), i, {"replica": other})
+
+    right = mod(tx + 1, T)
+    left = mod(tx - 1, T)
+    fetched, missing = parity * HB, (1 - parity) * HB
+    QH2 = HB // 2
+    far_a = weight_piece(own_rows(opposite, fetched, QH2), relay.at[0], 0, {"tensor": right})
+    far_b = weight_piece(own_rows(opposite, fetched + QH2, QH2), relay.at[1], 1, {"tensor": left})
+    near_a = weight_piece(own_rows(right, fetched, HB), held(tx, fetched, HB), 2, {"tensor": right})
+    near_b = weight_piece(own_rows(left, fetched, HB), held(tx, fetched, HB), 3, {"tensor": left})
+    pass_a = weight_piece(relay.at[0], held(left, fetched, QH2), 4, {"tensor": right})
+    pass_b = weight_piece(relay.at[1], held(right, fetched + QH2, QH2), 5, {"tensor": left})
+    owners = (left, right, opposite)
+    spread = [
+        [same_place(owner, fetched + e * QB, QB, 6 + 4 * j + e, around[e]) for e in range(4)]
+        for j, owner in enumerate(owners)
+    ]
+    to_mate = [same_place(owner, fetched, HB, 18 + j, mate) for j, owner in enumerate(owners)]
+    rest_to_mate = [same_place(owner, missing, HB, 21 + j, mate) for j, owner in enumerate(owners)]
 
     def weight_copies(c):
         rows = pl.ds(pl.multiple_of(c * KC, KC), KC)
@@ -75,8 +130,6 @@
         return carry
 
     lax.fori_loop(1, R, greet, 0)
-    right = mod(tx + 1, T)
-    left = mod(tx - 1, T)
     for other in (right, left):
         pl.semaphore_signal(barrier, inc=1, device_id={"tensor": other}, device_id_type=MESH)
 
@@ -91,6 +144,8 @@
         meta_out[n] = jnp.broadcast_to(codes[n : n + 1], (8, 128))
 
     pl.semaphore_wait(barrier, R - 1 + 2)
+    far_a.start()
+    far_b.start()
 
     def to_all(make):
         def send(k, carry):
@@ -147,6 +202,8 @@
     early = chunks // 2
     for c in range(early):
         project(c)
+    near_a.start()
+    near_b.start()
 
     settle(meta_in.at[pl.ds(0, R - 1)], meta_recv)
     meta_in[me] = meta_out[me]
@@ -202,8 +259,14 @@
 
     to_all(q_copy)
     q_in[me] = q_out[me]
-    wo_copy = pltpu.make_async_copy(wo_hbm, wo, wo_sem)
+    wo_copy = pltpu.make_async_copy(
+        wo_hbm.at[:, pl.ds(pl.multiple_of(tx * DC, 128), DC)], wf.at[rows_at(tx, 0, KR)], wo_sem
+    )
     wo_copy.start()
+    far_a.wait_recv()
+    pass_a.start()
+    far_b.wait_recv()
+    pass_b.start()
 
     per = 128 // MSG
     group_of_lane = lax.broadcasted_iota(jnp.int32, (8, 128), 1) // MSG
@@ -288,89 +351,97 @@
 
         return carry
 
-    lax.fori_loop(0, groups, attend_group, 0, unroll=2)
+    lax.fori_loop(0, groups // 2, attend_group, 0, unroll=2)
+    near_a.wait_recv()
+    near_b.wait_recv()
+    for j in (0, 1):
+        to_mate[j].start()
+        for e in range(4):
+            spread[j][e].start()
+    lax.fori_loop(groups // 2, groups, attend_group, 0, unroll=2)
     h_in[me] = h_out[me]
-
-    wo_copy.wait()
+    pass_a.wait_recv()
+    pass_b.wait_recv()
+    to_mate[2].start()
+    for e in range(4):
+        spread[2][e].start()
+
     settle(h_in.at[pl.ds(0, R - 1)], h_recv)
     flat = h_in[...].reshape(R * MSG, HD)
     by_head = jnp.dot(unpick[...], flat, preferred_element_type=F32).astype(BF16)
     for h in range(NQ):
-        heads[:, h * HD : (h + 1) * HD] = by_head[h * M : (h + 1) * M]
-
-    wide = DC // SUBS
-
-    def cols_of(c, b):
-        return pl.ds(pl.multiple_of(c * DC + b * wide, 128), wide)
-
-    def partial(c, b):
-        return jnp.dot(heads[...], wo[:, cols_of(c, b)], preferred_element_type=F32)
-
-    def push(src, dst, b, i, other):
+        heads[tx, :, h * HD : (h + 1) * HD] = by_head[h * M : (h + 1) * M]
+
+    def push(ref, i, other):
         copy = pltpu.make_async_remote_copy(
-            src_ref=src, dst_ref=dst, send_sem=x_send.at[b, i], recv_sem=x_recv.at[b, i],
+            src_ref=ref, dst_ref=ref, send_sem=x_send.at[i], recv_sem=x_recv.at[i],
             device_id={"tensor": other}, device_id_type=MESH,
         )
         copy.start()
         return copy
 
-    low, high = slice(0, half), slice(half, M)
-    subs = range(SUBS)
-    c0, c1, c2, c3, c4, c5, c6, c7, c8, c9 = ([] for _ in range(10))
-    for b in subs:
-        far[b] = partial(mod(tx + 2, T), b).astype(BF16)
-        c0.append(push(far.at[b, low], got.at[b, 0], b, 0, right))
-        c1.append(push(far.at[b, high], got.at[b, 1], b, 1, left))
-    for b in subs:
-        sums_r[b] = partial(right, b)
-        near_r[b, high] = sums_r[b, high].astype(BF16)
-        sums_l[b] = partial(left, b)
-        near_l[b, low] = sums_l[b, low].astype(BF16)
-    for b in subs:
-        part[b] = partial(tx, b)
-    for b in subs:
-        c0[b].wait_send()
-        c2.append(push(near_r.at[b, high], got.at[b, 2], b, 2, right))
-        c1[b].wait_send()
-        c3.append(push(near_l.at[b, low], got.at[b, 3], b, 3, left))
-    for b in subs:
-        c0[b].wait_recv()
-        near_r[b, low] = (sums_r[b, low] + got[b, 0].astype(F32)).astype(BF16)
-        c2[b].wait_send()
-        c4.append(push(near_r.at[b, low], got.at[b, 4], b, 4, right))
-        c1[b].wait_recv()
-        near_l[b, high] = (sums_l[b, high] + got[b, 1].astype(F32)).astype(BF16)
-        c3[b].wait_send()
-        c5.append(push(near_l.at[b, high], got.at[b, 5], b, 5, left))
-    own = []
-    for b in subs:
-        mine = out_hbm.at[:, cols_of(tx, b)]
-        c3[b].wait_recv()
-        c4[b].wait_recv()
-        final[b, low] = (part[b, low] + got[b, 3].astype(F32) + got[b, 4].astype(F32)).astype(BF16)
-        c6.append(push(final.at[b, low], mine.at[low], b, 6, right))
-        c2[b].wait_recv()
-        c5[b].wait_recv()
-        final[b, high] = (part[b, high] + got[b, 2].astype(F32) + got[b, 5].astype(F32)).astype(BF16)
-        c7.append(push(final.at[b, high], mine.at[high], b, 7, left))
-        c8.append(push(final.at[b, high], mine.at[high], b, 8, right))
-        c9.append(push(final.at[b, low], mine.at[low], b, 9, left))
-        own.append(pltpu.make_async_copy(final.at[b], mine, out_sem.at[b]))
-        own[b].start()
-    last = []
-    for b in subs:
-        from_left = out_hbm.at[low, cols_of(left, b)]
-        from_right = out_hbm.at[high, cols_of(right, b)]
-        c6[b].wait_recv()
-        last.append(push(from_left, from_left, b, 10, right))
-        c7[b].wait_recv()
-        last.append(push(from_right, from_right, b, 11, left))
-    for copy in c8 + c9 + last:
+    low, high = pl.ds(0, half), pl.ds(half, half)
+    g0 = push(heads.at[tx, low], 0, right)
+    g1 = push(heads.at[tx, high], 1, left)
+    g2 = push(heads.at[tx, high], 2, right)
+    g3 = push(heads.at[tx, low], 3, left)
+
+    def term(owner, cols):
+        rows = pl.ds(pl.multiple_of(owner * KR, 16), KR)
+        return jnp.dot(heads[owner], wf[rows, cols], preferred_element_type=F32)
+
+    every = slice(0, DC)
+    wo_copy.wait()
+    total[...] = term(tx, every)
+    for j in range(3):
+        for e in range(4):
+            spread[j][e].wait_recv()
+        rest_to_mate[j].start()
+    g0.wait_recv()
+    g4 = push(heads.at[left, low], 4, right)
+    g1.wait_recv()
+    g5 = push(heads.at[right, high], 5, left)
+    g2.wait_recv()
+    to_mate[0].wait_recv()
+    rest_to_mate[0].wait_recv()
+    total[...] += term(left, every)
+    g3.wait_recv()
+    to_mate[1].wait_recv()
+    rest_to_mate[1].wait_recv()
+    total[...] += term(right, every)
+    to_mate[2].wait_recv()
+    rest_to_mate[2].wait_recv()
+    g4.wait_recv()
+    g5.wait_recv()
+
+    wide = DC // SUBS
+
+    def cols_of(owner, b):
+        return pl.ds(pl.multiple_of(owner * DC + b * wide, 128), wide)
+
+    done = [g0, g1, g2, g3, g4, g5]
+    first_r, first_l, second = [], [], []
+    for b in range(SUBS):
+        part = slice(b * wide, (b + 1) * wide)
+        mine = cols_of(tx, b)
+        out_ref[:, mine] = (total[:, part] + term(opposite, part)).astype(BF16)
+        i = 6 + 6 * b
+        first_r.append(push(out_ref.at[low, mine], i, right))
+        first_l.append(push(out_ref.at[high, mine], i + 1, left))
+        second.append(push(out_ref.at[high, mine], i + 2, right))
+        second.append(push(out_ref.at[low, mine], i + 3, left))
+    for b in range(SUBS):
+        i = 6 + 6 * b
+        first_r[b].wait_recv()
+        second.append(push(out_ref.at[low, cols_of(left, b)], i + 4, right))
+        first_l[b].wait_recv()
+        second.append(push(out_ref.at[high, cols_of(right, b)], i + 5, left))
+    for copy in second:
         copy.wait_recv()
-    for copy in c4 + c5 + c6 + c7 + c8 + c9 + last:
+    for copy in done + first_r + first_l + second:
         copy.wait_send()
-    for copy in own:
-        copy.wait()
+    for copy in [far_a, far_b, near_a, near_b, pass_a, pass_b] + sum(spread, []) + to_mate + rest_to_mate:
+        copy.wait_send()
     some = pl.ds(0, R - 1)
     settle(meta_out.at[some], meta_send)
     settle(q_out.at[some], q_send)
@@ -393,16 +464,17 @@
     dma = pltpu.SemaphoreType.DMA
     out = pl.pallas_call(
         functools.partial(kernel, (R, T, S, NQ, D, KC)),
-        out_shape=jax.ShapeDtypeStruct((M, D), BF16),
+        out_shape=pltpu.VMEM((M, D), BF16),
         in_specs=[smem, smem, smem, pl.BlockSpec(memory_space=pltpu.VMEM)] + [any_spec] * 6,
-        out_specs=any_spec,
+        out_specs=pl.BlockSpec(memory_space=pltpu.VMEM),
         scratch_shapes=[
             pltpu.VMEM((M, D), BF16),
             pltpu.VMEM((D, NQ * HD), BF16),
             pltpu.VMEM((D, HD), BF16),
             pltpu.VMEM((D, HD), BF16),
             pltpu.VMEM(kv_pages.shape, BF16),
-            pltpu.VMEM(w_out.shape, BF16),
+            pltpu.VMEM((T * w_out.shape[0], DC), BF16),
+            pltpu.VMEM((2, w_out.shape[0] // 4, DC // 2), BF16),
             pltpu.VMEM((M, NH * HD), F32),
             pltpu.VMEM((R, 128), jnp.int32),
             pltpu.SMEM((R, 128), jnp.int32),
@@ -415,17 +487,10 @@
             pltpu.VMEM((R, MSG, HD), BF16),
             pltpu.VMEM((R, MSG, HD), BF16),
             pltpu.VMEM((R, MSG, HD), BF16),
-            pltpu.VMEM((M, NQ * HD), BF16),
-            pltpu.VMEM((SUBS, M, DC // SUBS), F32),
-            pltpu.VMEM((SUBS, M, DC // SUBS), F32),
-            pltpu.VMEM((SUBS, M, DC // SUBS), F32),
-            pltpu.VMEM((SUBS, M, DC // SUBS), BF16),
-            pltpu.VMEM((SUBS, M, DC // SUBS), BF16),
-            pltpu.VMEM((SUBS, M, DC // SUBS), BF16),
-            pltpu.VMEM((SUBS, 6, M // 2, DC // SUBS), BF16),
-            pltpu.VMEM((SUBS, M, DC // SUBS), BF16),
+            pltpu.VMEM((T, M, NQ * HD), BF16),
+            pltpu.VMEM((M, DC), F32),
             dma, dma((D // KC, 3)), dma((4,)), dma, dma,
-            dma, dma, dma, dma((R,)), dma, dma, dma((SUBS, 12)), dma((SUBS, 12)), dma((SUBS,)),
+            dma, dma, dma, dma((R,)), dma, dma, dma((6 + 6 * SUBS,)), dma((6 + 6 * SUBS,)), dma((24,)), dma((24,)),
         ],
         compiler_params=pltpu.CompilerParams(
             collective_id=0, has_side_effects=True, vmem_limit_bytes=58 * 1024 * 1024

time: 58.1 us -> 58.6 us (level)
  Pallas kernels: 55.4 us -> 57.4 us
  local copies, waits for them, and re-layouts: 2.46 us -> 1.06 us
    pallas_call x1, Pallas kernels: 55.4 us -> 57.4 us  [shards(): pl.pallas_call(functools.partial(kernel, (R, T, S, NQ, D, KC)), out_shape...]
    unnamed x1, local copies, waits for them, and re-layouts: 2.46 us -> 1.06 us
where the time goes in v5:
time: 58.6 us; the launch traced here: 58.5 us
  Pallas kernels  57.4 us (98%)
  local copies, waits for them, and re-layouts  1.06 us (2%)
    pallas_call x1, Pallas kernels, shards(): pl.pallas_call(functools.partial(kernel, (R, T, S, NQ, D, KC)), out_shape...  57.4 us

profile of v5, /device:TPU:0, one launch (start us, length us, event | category | flops | bytes accessed | tf_op | source)
XLA Modules:
  0.0 58.5 jit_solution(4718247006914354564)
XLA Ops:
  0.0 57.4 %decode_attention.1 = bf16[128,5120]{1,0:T(8,128)(2,1)S(1)} custom-call(s32[32]{0:T(128)} %dest_sm.1, s32[32]{0:T(128)} %len_sm.1, s32[4,32]{1,0:T(4,128)} %bitcast.7, f32[1,5120]{1,0:T(1,128)} %bitcast.6, bf16[128,5120]{1,0:T(8,128)(2,1)} %bitcast.5, bf16[5120,640]{1,0:T(8,128)(2,1)} %wq_hbm.1, bf16[5120,128]{1,0:T(8,128)(2,1)} %wk_hbm.1, ...), custom_call_target="tpu_custom_call" | custom-call | tf_op jit(solution)/shard_map/decode_attention/pallas_call | solution.py:465
  57.4 1.1 %copy.12 = bf16[4,32,5120]{2,1,0:T(8,128)(2,1)} copy(bf16[4,32,5120]{2,1,0:T(8,128)(2,1)S(1)} %bitcast.4) | data formatting | bytes 2621440

commit v6 on v5

--- a/solution.py
+++ b/solution.py
@@ -144,8 +144,8 @@
         meta_out[n] = jnp.broadcast_to(codes[n : n + 1], (8, 128))
 
     pl.semaphore_wait(barrier, R - 1 + 2)
-    far_a.start()
-    far_b.start()
+    near_a.start()
+    near_b.start()
 
     def to_all(make):
         def send(k, carry):
@@ -202,8 +202,8 @@
     early = chunks // 2
     for c in range(early):
         project(c)
-    near_a.start()
-    near_b.start()
+    far_a.start()
+    far_b.start()
 
     settle(meta_in.at[pl.ds(0, R - 1)], meta_recv)
     meta_in[me] = meta_out[me]
@@ -263,10 +263,12 @@
         wo_hbm.at[:, pl.ds(pl.multiple_of(tx * DC, 128), DC)], wf.at[rows_at(tx, 0, KR)], wo_sem
     )
     wo_copy.start()
-    far_a.wait_recv()
-    pass_a.start()
-    far_b.wait_recv()
-    pass_b.start()
+    near_a.wait_recv()
+    near_b.wait_recv()
+    for j in (0, 1):
+        to_mate[j].start()
+        for e in range(4):
+            spread[j][e].start()
 
     per = 128 // MSG
     group_of_lane = lax.broadcasted_iota(jnp.int32, (8, 128), 1) // MSG
@@ -285,6 +287,10 @@
 
     span = max_pages * page
     rows = GROUP * MSG
+    far_a.wait_recv()
+    pass_a.start()
+    far_b.wait_recv()
+    pass_b.start()
     tok = lax.broadcasted_iota(jnp.int32, (MSG, span), 1)
     f_row = lax.broadcasted_iota(jnp.int32, (rows, rows), 0)
     f_col = lax.broadcasted_iota(jnp.int32, (rows, rows), 1)
@@ -352,19 +358,15 @@
         return carry
 
     lax.fori_loop(0, groups // 2, attend_group, 0, unroll=2)
-    near_a.wait_recv()
-    near_b.wait_recv()
     for j in (0, 1):
-        to_mate[j].start()
         for e in range(4):
-            spread[j][e].start()
+            spread[j][e].wait_recv()
+        rest_to_mate[j].start()
     lax.fori_loop(groups // 2, groups, attend_group, 0, unroll=2)
     h_in[me] = h_out[me]
     pass_a.wait_recv()
     pass_b.wait_recv()
     to_mate[2].start()
-    for e in range(4):
-        spread[2][e].start()
 
     settle(h_in.at[pl.ds(0, R - 1)], h_recv)
     flat = h_in[...].reshape(R * MSG, HD)
@@ -385,6 +387,8 @@
     g1 = push(heads.at[tx, high], 1, left)
     g2 = push(heads.at[tx, high], 2, right)
     g3 = push(heads.at[tx, low], 3, left)
+    for e in range(4):
+        spread[2][e].start()
 
     def term(owner, cols):
         rows = pl.ds(pl.multiple_of(owner * KR, 16), KR)
@@ -393,10 +397,9 @@
     every = slice(0, DC)
     wo_copy.wait()
     total[...] = term(tx, every)
-    for j in range(3):
-        for e in range(4):
-            spread[j][e].wait_recv()
-        rest_to_mate[j].start()
+    for e in range(4):
+        spread[2][e].wait_recv()
+    rest_to_mate[2].start()
     g0.wait_recv()
     g4 = push(heads.at[left, low], 4, right)
     g1.wait_recv()

time: 58.6 us -> 56.9 us (0.971)
  Pallas kernels: 57.4 us -> 55.6 us
    pallas_call x1, Pallas kernels: 57.4 us -> 55.6 us  [shards(): pl.pallas_call(functools.partial(kernel, (R, T, S, NQ, D, KC)), out_shape...]
where the time goes in v6:
time: 56.9 us; the launch traced here: 56.6 us
  Pallas kernels  55.6 us (98%)
  local copies, waits for them, and re-layouts  1.06 us (2%)
    pallas_call x1, Pallas kernels, shards(): pl.pallas_call(functools.partial(kernel, (R, T, S, NQ, D, KC)), out_shape...  55.6 us

profile of v6, /device:TPU:0, one launch (start us, length us, event | category | flops | bytes accessed | tf_op | source)
XLA Modules:
  0.0 56.6 jit_solution(5376610925447879116)
XLA Ops:
  0.0 55.6 %decode_attention.1 = bf16[128,5120]{1,0:T(8,128)(2,1)S(1)} custom-call(s32[32]{0:T(128)} %dest_sm.1, s32[32]{0:T(128)} %len_sm.1, s32[4,32]{1,0:T(4,128)} %bitcast.7, f32[1,5120]{1,0:T(1,128)} %bitcast.6, bf16[128,5120]{1,0:T(8,128)(2,1)} %bitcast.5, bf16[5120,640]{1,0:T(8,128)(2,1)} %wq_hbm.1, bf16[5120,128]{1,0:T(8,128)(2,1)} %wk_hbm.1, ...), custom_call_target="tpu_custom_call" | custom-call | tf_op jit(solution)/shard_map/decode_attention/pallas_call | solution.py:468
  55.6 1.1 %copy.12 = bf16[4,32,5120]{2,1,0:T(8,128)(2,1)} copy(bf16[4,32,5120]{2,1,0:T(8,128)(2,1)S(1)} %bitcast.4) | data formatting | bytes 2621440

commit v7 on v6

--- a/solution.py
+++ b/solution.py
@@ -32,7 +32,7 @@
     sizes,
     dest_sm, len_sm, table_sm, gain_ref, hid_hbm, wq_hbm, wk_hbm, wv_hbm, wo_hbm, kv_hbm,
     out_ref,
-    hid, wq, wk, wv, kv, wf, relay, acc, code, code_sm, meta_out, meta_in, pick, unpick, stack,
+    hid, wq, wk, wv, kv, wf, relay, acc, code, code_sm, meta_out, meta_in, unpick, by_head, stack,
     q_out, q_in, h_out, h_in, heads, total,
     hid_sem, w_sem, kv_sem, wo_sem, code_sem,
     meta_send, meta_recv, q_send, q_recv, h_send, h_recv, x_send, x_recv, f_send, f_recv,
@@ -93,10 +93,18 @@
     QH2 = HB // 2
     far_a = weight_piece(own_rows(opposite, fetched, QH2), relay.at[0], 0, {"tensor": right})
     far_b = weight_piece(own_rows(opposite, fetched + QH2, QH2), relay.at[1], 1, {"tensor": left})
-    near_a = weight_piece(own_rows(right, fetched, HB), held(tx, fetched, HB), 2, {"tensor": right})
-    near_b = weight_piece(own_rows(left, fetched, HB), held(tx, fetched, HB), 3, {"tensor": left})
-    pass_a = weight_piece(relay.at[0], held(left, fetched, QH2), 4, {"tensor": right})
-    pass_b = weight_piece(relay.at[1], held(right, fetched + QH2, QH2), 5, {"tensor": left})
+    near_a, near_b = (
+        [
+            weight_piece(
+                own_rows(target, fetched + p * QH2, QH2), held(tx, fetched + p * QH2, QH2), 2 + 2 * p + i,
+                {"tensor": target},
+            )
+            for p in range(2)
+        ]
+        for i, target in enumerate((right, left))
+    )
+    pass_a = weight_piece(relay.at[0], held(left, fetched, QH2), 24, {"tensor": right})
+    pass_b = weight_piece(relay.at[1], held(right, fetched + QH2, QH2), 25, {"tensor": left})
     owners = (left, right, opposite)
     spread = [
         [same_place(owner, fetched + e * QB, QB, 6 + 4 * j + e, around[e]) for e in range(4)]
@@ -121,17 +129,22 @@
                 copy.start()
 
     load(0)
-    load(1)
 
     barrier = pltpu.get_barrier_semaphore()
 
+    def far_first(k):
+        return R // 2 + (1 - 2 * (k % 2)) * ((k + 1) // 2)
+
     def greet(k, carry):
-        pl.semaphore_signal(barrier, inc=1, device_id={"replica": mod(me + k, R)}, device_id_type=MESH)
+        n = mod(me + far_first(k), R)
+        pl.semaphore_signal(barrier, inc=1, device_id={"replica": n}, device_id_type=MESH)
         return carry
 
-    lax.fori_loop(1, R, greet, 0)
+    lax.fori_loop(0, R - 1, greet, 0)
     for other in (right, left):
         pl.semaphore_signal(barrier, inc=1, device_id={"tensor": other}, device_id_type=MESH)
+
+    load(1)
 
     numbers = lax.broadcasted_iota(jnp.int32, (R, 128), 0)
     codes = jnp.zeros((R, 128), jnp.int32)
@@ -144,8 +157,6 @@
         meta_out[n] = jnp.broadcast_to(codes[n : n + 1], (8, 128))
 
     pl.semaphore_wait(barrier, R - 1 + 2)
-    near_a.start()
-    near_b.start()
 
     def to_all(make):
         def send(k, carry):
@@ -165,7 +176,13 @@
             device_id={"replica": n}, device_id_type=MESH,
         )
 
-    to_all(meta_copy)
+    def send_meta(k, carry):
+        meta_copy(mod(me + far_first(k), R)).start()
+        return carry
+
+    lax.fori_loop(0, R - 1, send_meta, 0)
+    far_a.start()
+    far_b.start()
 
     hid_copy.wait()
     load(2)
@@ -199,30 +216,32 @@
         term = jnp.dot(hid[:, cols], weights, preferred_element_type=F32)
         acc[...] = term if c == 0 else acc[...] + term
 
-    early = chunks // 2
-    for c in range(early):
+    for c in range(chunks):
         project(c)
-    far_a.start()
-    far_b.start()
-
+        if c == chunks // 2:
+            near_a[0].start()
+            near_b[0].start()
+
+    def share_near(p):
+        near_a[p].wait_recv()
+        near_b[p].wait_recv()
+        for j in (0, 1):
+            for e in (2 * p, 2 * p + 1):
+                spread[j][e].start()
+
+    near_a[1].start()
+    near_b[1].start()
     settle(meta_in.at[pl.ds(0, R - 1)], meta_recv)
     meta_in[me] = meta_out[me]
 
     slot_rows = lax.broadcasted_iota(jnp.int32, (R, 128), 0)
     lens = jnp.zeros((R, 128), jnp.int32)
-    msg_row = lax.broadcasted_iota(jnp.int32, (MSG, 128), 0)
-    lane = lax.broadcasted_iota(jnp.int32, (MSG, 128), 1)
     for o in range(R):
         tile = meta_in[o]
-        slot = tile & (R - 1)
-        slot_wide = jnp.concatenate([slot] * (R // 8), 0)
+        slot_wide = jnp.concatenate([tile & (R - 1)] * (R // 8), 0)
         len_wide = jnp.concatenate([lax.shift_right_logical(tile, int(math.log2(R)))] * (R // 8), 0)
         lens = jnp.where(slot_rows == slot_wide, len_wide, lens)
-        target = R * msg_row + jnp.concatenate([slot] * (MSG // 8), 0)
-        for c in range(0, NH * M, 128):
-            width = min(128, NH * M - c)
-            hit = jnp.where(target == lane + c, 1.0, 0.0).astype(BF16)
-            pick[pl.ds(o * MSG, MSG), c : c + width] = hit[:, :width]
+
     freq_lane = lax.broadcasted_iota(jnp.int32, (8, 128), 1) % (HD // 2)
     freq = jnp.exp(freq_lane.astype(F32) * (-2.0 / HD * math.log(ROPE_BASE)))
     angle = lens.astype(F32) * jnp.concatenate([freq] * (R // 8), 0)
@@ -241,15 +260,12 @@
     cosine = jnp.concatenate(cosines, 0)
     sine = jnp.concatenate(sines, 0)
 
-    for c in range(early, chunks):
-        project(c)
 
     for h in range(NH):
         vec = acc[:, h * HD : (h + 1) * HD]
         if h <= NQ:
             vec = vec * cosine + pltpu.roll(vec, HD // 2, 1) * sine
         stack[h * M : (h + 1) * M, :] = vec.astype(BF16)
-    q_out[...] = jnp.dot(pick[...], stack[...], preferred_element_type=F32).astype(BF16).reshape(R, MSG, HD)
 
     def q_copy(o):
         return pltpu.make_async_remote_copy(
@@ -257,19 +273,37 @@
             device_id={"replica": o}, device_id_type=MESH,
         )
 
-    to_all(q_copy)
+    msg_row = lax.broadcasted_iota(jnp.int32, (MSG, 128), 0)
+    lane = lax.broadcasted_iota(jnp.int32, (MSG, 128), 1)
+
+    def send_group(i, carry):
+        first = mod(group + 1 + i, groups) * GROUP
+        blocks = []
+        for u in range(GROUP):
+            slot = meta_in[first + u] & (R - 1)
+            target = R * msg_row + jnp.concatenate([slot] * (MSG // 8), 0)
+            parts = []
+            for c in range(0, NH * M, 128):
+                hit = jnp.where(target == lane + c, 1.0, 0.0).astype(BF16)
+                parts.append(hit[:, : min(128, NH * M - c)])
+            blocks.append(jnp.concatenate(parts, 1))
+        pick = jnp.concatenate(blocks, 0)
+        rows = jnp.dot(pick, stack[...], preferred_element_type=F32)
+        q_out[pl.ds(first, GROUP)] = rows.astype(BF16).reshape(GROUP, MSG, HD)
+        for u in range(GROUP):
+
+            @pl.when(first + u != me)
+            def _():
+                q_copy(first + u).start()
+
+        return carry
+
+    lax.fori_loop(0, groups, send_group, 0, unroll=2)
     q_in[me] = q_out[me]
     wo_copy = pltpu.make_async_copy(
         wo_hbm.at[:, pl.ds(pl.multiple_of(tx * DC, 128), DC)], wf.at[rows_at(tx, 0, KR)], wo_sem
     )
     wo_copy.start()
-    near_a.wait_recv()
-    near_b.wait_recv()
-    for j in (0, 1):
-        to_mate[j].start()
-        for e in range(4):
-            spread[j][e].start()
-
     per = 128 // MSG
     group_of_lane = lax.broadcasted_iota(jnp.int32, (8, 128), 1) // MSG
     row_of_lane = lax.broadcasted_iota(jnp.int32, (8, 128), 1) % MSG
@@ -281,16 +315,16 @@
         target = jnp.concatenate([R * row_of_lane + slots] * (NQ * M // 8), 0)
         unpick[:, g * 128 : (g + 1) * 128] = jnp.where(target == wide_row, 1.0, 0.0).astype(BF16)
 
-    code_copy.wait()
-    for copy in kv_copies:
-        copy.wait()
-
-    span = max_pages * page
-    rows = GROUP * MSG
     far_a.wait_recv()
     pass_a.start()
     far_b.wait_recv()
     pass_b.start()
+    code_copy.wait()
+    for copy in kv_copies:
+        copy.wait()
+
+    span = max_pages * page
+    rows = GROUP * MSG
     tok = lax.broadcasted_iota(jnp.int32, (MSG, span), 1)
     f_row = lax.broadcasted_iota(jnp.int32, (rows, rows), 0)
     f_col = lax.broadcasted_iota(jnp.int32, (rows, rows), 1)
@@ -334,7 +368,7 @@
 
     def heads_copy(n):
         return pltpu.make_async_remote_copy(
-            src_ref=h_out.at[n], dst_ref=h_in.at[me], send_sem=h_send, recv_sem=h_recv,
+            src_ref=h_out.at[n], dst_ref=h_in.at[me], send_sem=h_send, recv_sem=h_recv.at[me],
             device_id={"replica": n}, device_id_type=MESH,
         )
 
@@ -357,22 +391,31 @@
 
         return carry
 
-    lax.fori_loop(0, groups // 2, attend_group, 0, unroll=2)
-    for j in (0, 1):
-        for e in range(4):
-            spread[j][e].wait_recv()
-        rest_to_mate[j].start()
-    lax.fori_loop(groups // 2, groups, attend_group, 0, unroll=2)
+    lax.fori_loop(0, groups, attend_group, 0, unroll=2)
     h_in[me] = h_out[me]
-    pass_a.wait_recv()
-    pass_b.wait_recv()
-    to_mate[2].start()
-
-    settle(h_in.at[pl.ds(0, R - 1)], h_recv)
-    flat = h_in[...].reshape(R * MSG, HD)
-    by_head = jnp.dot(unpick[...], flat, preferred_element_type=F32).astype(BF16)
+    share_near(0)
+    share_near(1)
+    to_mate[0].start()
+    to_mate[1].start()
+    def collect(i, carry):
+        g = mod(group + 1 + i, groups)
+        for u in range(GROUP):
+            n = g * GROUP + u
+
+            @pl.when(n != me)
+            def _():
+                settle(h_in.at[n], h_recv.at[n])
+
+        flat = h_in[pl.ds(g * GROUP, GROUP)].reshape(GROUP * MSG, HD)
+        cols = pl.ds(pl.multiple_of(g * 128, 128), 128)
+        rows = jnp.dot(unpick[:, cols], flat, preferred_element_type=F32)
+        by_head[...] += rows
+        return carry
+
+    by_head[...] = jnp.zeros_like(by_head)
+    lax.fori_loop(0, groups, collect, 0)
     for h in range(NQ):
-        heads[tx, :, h * HD : (h + 1) * HD] = by_head[h * M : (h + 1) * M]
+        heads[tx, :, h * HD : (h + 1) * HD] = by_head[h * M : (h + 1) * M].astype(BF16)
 
     def push(ref, i, other):
         copy = pltpu.make_async_remote_copy(
@@ -387,6 +430,9 @@
     g1 = push(heads.at[tx, high], 1, left)
     g2 = push(heads.at[tx, high], 2, right)
     g3 = push(heads.at[tx, low], 3, left)
+    pass_a.wait_recv()
+    pass_b.wait_recv()
+    to_mate[2].start()
     for e in range(4):
         spread[2][e].start()
 
@@ -397,6 +443,10 @@
     every = slice(0, DC)
     wo_copy.wait()
     total[...] = term(tx, every)
+    for j in (0, 1):
+        for e in range(4):
+            spread[j][e].wait_recv()
+        rest_to_mate[j].start()
     for e in range(4):
         spread[2][e].wait_recv()
     rest_to_mate[2].start()
@@ -443,7 +493,7 @@
         copy.wait_recv()
     for copy in done + first_r + first_l + second:
         copy.wait_send()
-    for copy in [far_a, far_b, near_a, near_b, pass_a, pass_b] + sum(spread, []) + to_mate + rest_to_mate:
+    for copy in [far_a, far_b, pass_a, pass_b] + near_a + near_b + sum(spread, []) + to_mate + rest_to_mate:
         copy.wait_send()
     some = pl.ds(0, R - 1)
     settle(meta_out.at[some], meta_send)
@@ -483,8 +533,8 @@
             pltpu.SMEM((R, 128), jnp.int32),
             pltpu.VMEM((R, 8, 128), jnp.int32),
             pltpu.VMEM((R, 8, 128), jnp.int32),
-            pltpu.VMEM((R * MSG, NH * M), BF16),
             pltpu.VMEM((NQ * M, R * MSG), BF16),
+            pltpu.VMEM((NQ * M, HD), F32),
             pltpu.VMEM((NH * M, HD), BF16),
             pltpu.VMEM((R, MSG, HD), BF16),
             pltpu.VMEM((R, MSG, HD), BF16),
@@ -493,7 +543,7 @@
             pltpu.VMEM((T, M, NQ * HD), BF16),
             pltpu.VMEM((M, DC), F32),
             dma, dma((D // KC, 3)), dma((4,)), dma, dma,
-            dma, dma, dma, dma((R,)), dma, dma, dma((6 + 6 * SUBS,)), dma((6 + 6 * SUBS,)), dma((24,)), dma((24,)),
+            dma, dma, dma, dma((R,)), dma, dma((R,)), dma((6 + 6 * SUBS,)), dma((6 + 6 * SUBS,)), dma((26,)), dma((26,)),
         ],
         compiler_params=pltpu.CompilerParams(
             collective_id=0, has_side_effects=True, vmem_limit_bytes=58 * 1024 * 1024

time: 56.9 us -> 52.1 us (0.916)
  Pallas kernels: 55.6 us -> 50.8 us
    pallas_call x1, Pallas kernels: 55.6 us -> 50.8 us  [shards(): pl.pallas_call(functools.partial(kernel, (R, T, S, NQ, D, KC)), out_shape...]
where the time goes in v7:
time: 52.1 us; the launch traced here: 51.9 us
  Pallas kernels  50.8 us (98%)
  local copies, waits for them, and re-layouts  1.06 us (2%)
    pallas_call x1, Pallas kernels, shards(): pl.pallas_call(functools.partial(kernel, (R, T, S, NQ, D, KC)), out_shape...  50.8 us
    unnamed x1, local copies, waits for them, and re-layouts  1.06 us

profile of v7, /device:TPU:0, one launch (start us, length us, event | category | flops | bytes accessed | tf_op | source)
XLA Modules:
  0.0 51.9 jit_solution(2836941718526673205)
XLA Ops:
  0.0 50.8 %decode_attention.1 = bf16[128,5120]{1,0:T(8,128)(2,1)S(1)} custom-call(s32[32]{0:T(128)} %dest_sm.1, s32[32]{0:T(128)} %len_sm.1, s32[4,32]{1,0:T(4,128)} %bitcast.7, f32[1,5120]{1,0:T(1,128)} %bitcast.6, bf16[128,5120]{1,0:T(8,128)(2,1)} %bitcast.5, bf16[5120,640]{1,0:T(8,128)(2,1)} %wq_hbm.1, bf16[5120,128]{1,0:T(8,128)(2,1)} %wk_hbm.1, ...), custom_call_target="tpu_custom_call" | custom-call | tf_op jit(solution)/shard_map/decode_attention/pallas_call | solution.py:518
  50.9 1.1 %copy.12 = bf16[4,32,5120]{2,1,0:T(8,128)(2,1)} copy(bf16[4,32,5120]{2,1,0:T(8,128)(2,1)S(1)} %bitcast.4) | data formatting | bytes 2621440

commit v8 on v7

--- a/solution.py
+++ b/solution.py
@@ -13,7 +13,6 @@
 MSG = 32
 ROPE_BASE = 1000000.0
 EPSILON = 1e-06
-SUBS = 2
 CHIPS_Z = 4
 MESH = pl.DeviceIdType.MESH
 F32 = jnp.float32
@@ -30,9 +29,10 @@
 
 def kernel(
     sizes,
-    dest_sm, len_sm, table_sm, gain_ref, hid_hbm, wq_hbm, wk_hbm, wv_hbm, wo_hbm, kv_hbm,
+    dest_hbm, len_hbm, table_hbm, gain_hbm, hid_hbm, wq_hbm, wk_hbm, wv_hbm, wo_hbm, kv_hbm,
     out_ref,
-    hid, wq, wk, wv, kv, wf, relay, acc, code, code_sm, meta_out, meta_in, unpick, by_head, stack,
+    dest_sm, len_sm, table_sm, gain_ref, small_sem,
+    hid, wq, wk, wv, kv, wf, relay, acc, code, code_sm, meta_out, meta_in, order, unpick, gathered, stack,
     q_out, q_in, h_out, h_in, heads, total,
     hid_sem, w_sem, kv_sem, wo_sem, code_sem,
     meta_send, meta_recv, q_send, q_recv, h_send, h_recv, x_send, x_recv, f_send, f_recv,
@@ -111,7 +111,10 @@
         for j, owner in enumerate(owners)
     ]
     to_mate = [same_place(owner, fetched, HB, 18 + j, mate) for j, owner in enumerate(owners)]
-    rest_to_mate = [same_place(owner, missing, HB, 21 + j, mate) for j, owner in enumerate(owners)]
+    rest_to_mate = [
+        [same_place(owner, missing + e * QB, QB, 26 + 4 * j + e, mate) for e in range(4)]
+        for j, owner in enumerate(owners)
+    ]
 
     def weight_copies(c):
         rows = pl.ds(pl.multiple_of(c * KC, KC), KC)
@@ -121,6 +124,14 @@
             pltpu.make_async_copy(wv_hbm.at[rows], wv.at[rows], w_sem.at[c, 2]),
         )
 
+    small = [
+        pltpu.make_async_copy(src, dst, small_sem.at[i])
+        for i, (src, dst) in enumerate(
+            ((dest_hbm, dest_sm), (len_hbm, len_sm), (gain_hbm, gain_ref), (table_hbm, table_sm))
+        )
+    ]
+    for copy in small:
+        copy.start()
     hid_copy = pltpu.make_async_copy(hid_hbm, hid, hid_sem)
     hid_copy.start()
     def load(c):
@@ -146,6 +157,8 @@
 
     load(1)
 
+    small[0].wait()
+    small[1].wait()
     numbers = lax.broadcasted_iota(jnp.int32, (R, 128), 0)
     codes = jnp.zeros((R, 128), jnp.int32)
     for b in range(R):
@@ -185,6 +198,7 @@
     far_b.start()
 
     hid_copy.wait()
+    small[2].wait()
     load(2)
     squares = jnp.zeros((M, 128), F32)
     for c in range(D // 128):
@@ -304,22 +318,26 @@
         wo_hbm.at[:, pl.ds(pl.multiple_of(tx * DC, 128), DC)], wf.at[rows_at(tx, 0, KR)], wo_sem
     )
     wo_copy.start()
-    per = 128 // MSG
-    group_of_lane = lax.broadcasted_iota(jnp.int32, (8, 128), 1) // MSG
-    row_of_lane = lax.broadcasted_iota(jnp.int32, (8, 128), 1) % MSG
-    wide_row = lax.broadcasted_iota(jnp.int32, (NQ * M, 128), 0)
-    for g in range(R // per):
-        slots = jnp.zeros((8, 128), jnp.int32)
-        for i in range(per):
-            slots = jnp.where(group_of_lane == i, meta_in[g * per + i] & (R - 1), slots)
-        target = jnp.concatenate([R * row_of_lane + slots] * (NQ * M // 8), 0)
-        unpick[:, g * 128 : (g + 1) * 128] = jnp.where(target == wide_row, 1.0, 0.0).astype(BF16)
-
+    GS = GROUP * S
+    order_row = lax.broadcasted_iota(jnp.int32, (NQ * GS, GROUP * MSG), 0)
+    order_col = lax.broadcasted_iota(jnp.int32, (NQ * GS, GROUP * MSG), 1)
+    order_at = order_row % GS // S * MSG + order_row // GS * S + order_row % S
+    order[...] = jnp.where(order_at == order_col, 1.0, 0.0).astype(BF16)
+    arrival = lax.broadcasted_iota(jnp.int32, (8, M), 1)
+    slots = jnp.zeros((8, M), jnp.int32)
+    for k in range(R):
+        slot = meta_in[mod(group * GROUP + GROUP + k, R)][:, :M] & (R - 1)
+        slots = jnp.where(arrival // S == k, slot, slots)
+    slots = slots + R * (arrival % S)
+    wide_slots = jnp.concatenate([slots] * (M // 8), 0)
+    wide_rows = lax.broadcasted_iota(jnp.int32, (M, M), 0)
+    unpick[...] = jnp.where(wide_slots == wide_rows, 1.0, 0.0).astype(BF16)
     far_a.wait_recv()
     pass_a.start()
     far_b.wait_recv()
     pass_b.start()
     code_copy.wait()
+    small[3].wait()
     for copy in kv_copies:
         copy.wait()
 
@@ -397,103 +415,112 @@
     share_near(1)
     to_mate[0].start()
     to_mate[1].start()
-    def collect(i, carry):
-        g = mod(group + 1 + i, groups)
-        for u in range(GROUP):
-            n = g * GROUP + u
-
-            @pl.when(n != me)
-            def _():
-                settle(h_in.at[n], h_recv.at[n])
-
-        flat = h_in[pl.ds(g * GROUP, GROUP)].reshape(GROUP * MSG, HD)
-        cols = pl.ds(pl.multiple_of(g * 128, 128), 128)
-        rows = jnp.dot(unpick[:, cols], flat, preferred_element_type=F32)
-        by_head[...] += rows
-        return carry
-
-    by_head[...] = jnp.zeros_like(by_head)
-    lax.fori_loop(0, groups, collect, 0)
-    for h in range(NQ):
-        heads[tx, :, h * HD : (h + 1) * HD] = by_head[h * M : (h + 1) * M].astype(BF16)
-
     def push(ref, i, other):
         copy = pltpu.make_async_remote_copy(
             src_ref=ref, dst_ref=ref, send_sem=x_send.at[i], recv_sem=x_recv.at[i],
             device_id={"tensor": other}, device_id_type=MESH,
         )
         copy.start()
+        pushed.append(copy)
         return copy
 
-    low, high = pl.ds(0, half), pl.ds(half, half)
-    g0 = push(heads.at[tx, low], 0, right)
-    g1 = push(heads.at[tx, high], 1, left)
-    g2 = push(heads.at[tx, high], 2, right)
-    g3 = push(heads.at[tx, low], 3, left)
-    pass_a.wait_recv()
-    pass_b.wait_recv()
-    to_mate[2].start()
+    pushed = []
+    halves = range(2)
+    rows_of = [slice(v * half, (v + 1) * half) for v in halves]
+    span_of = [pl.ds(v * half, half) for v in halves]
+    to_right = [pl.ds(v * half, half // 2) for v in halves]
+    to_left = [pl.ds(v * half + half // 2, half // 2) for v in halves]
+
+    def collect(v):
+        for i in range(v * groups // 2, (v + 1) * groups // 2):
+            g = mod(group + 1 + i, groups)
+            for u in range(GROUP):
+                n = g * GROUP + u
+
+                @pl.when(n != me)
+                def _():
+                    settle(h_in.at[n], h_recv.at[n])
+
+            flat = h_in[pl.ds(g * GROUP, GROUP)].reshape(GROUP * MSG, HD)
+            rows = jnp.dot(order[...], flat, preferred_element_type=F32).astype(BF16)
+            for h in range(NQ):
+                heads[tx, i * GS : (i + 1) * GS, h * HD : (h + 1) * HD] = rows[h * GS : (h + 1) * GS]
+
+    heads_r, heads_l, heads_far = [], [], []
+    for v in halves:
+        collect(v)
+        heads_r.append(push(heads.at[tx, span_of[v]], 4 * v, right))
+        heads_l.append(push(heads.at[tx, span_of[v]], 4 * v + 1, left))
+        if v == 0:
+            pass_a.wait_recv()
+            pass_b.wait_recv()
+            to_mate[2].start()
+            for e in range(4):
+                spread[2][e].start()
+
+    def pass_heads(v):
+        heads_r[v].wait_recv()
+        heads_far.append(push(heads.at[left, to_right[v]], 4 * v + 2, right))
+        heads_l[v].wait_recv()
+        heads_far.append(push(heads.at[right, to_left[v]], 4 * v + 3, left))
+
+    def term(owner, rows):
+        block = wf[pl.ds(pl.multiple_of(owner * KR, 16), KR), :]
+        return jnp.dot(heads[owner, rows], block, preferred_element_type=F32)
+
+    pass_heads(0)
     for e in range(4):
-        spread[2][e].start()
-
-    def term(owner, cols):
-        rows = pl.ds(pl.multiple_of(owner * KR, 16), KR)
-        return jnp.dot(heads[owner], wf[rows, cols], preferred_element_type=F32)
-
-    every = slice(0, DC)
+        for j in (0, 1):
+            spread[j][e].wait_recv()
+            rest_to_mate[j][e].start()
     wo_copy.wait()
-    total[...] = term(tx, every)
-    for j in (0, 1):
-        for e in range(4):
-            spread[j][e].wait_recv()
-        rest_to_mate[j].start()
+    total[...] = term(tx, slice(0, M))
     for e in range(4):
         spread[2][e].wait_recv()
-    rest_to_mate[2].start()
-    g0.wait_recv()
-    g4 = push(heads.at[left, low], 4, right)
-    g1.wait_recv()
-    g5 = push(heads.at[right, high], 5, left)
-    g2.wait_recv()
-    to_mate[0].wait_recv()
-    rest_to_mate[0].wait_recv()
-    total[...] += term(left, every)
-    g3.wait_recv()
-    to_mate[1].wait_recv()
-    rest_to_mate[1].wait_recv()
-    total[...] += term(right, every)
+        rest_to_mate[2][e].start()
+    for j in (0, 1):
+        to_mate[j].wait_recv()
+        for e in range(4):
+            rest_to_mate[j][e].wait_recv()
+    total[rows_of[0]] += term(left, rows_of[0]) + term(right, rows_of[0])
+    pass_heads(1)
     to_mate[2].wait_recv()
-    rest_to_mate[2].wait_recv()
-    g4.wait_recv()
-    g5.wait_recv()
-
-    wide = DC // SUBS
-
-    def cols_of(owner, b):
-        return pl.ds(pl.multiple_of(owner * DC + b * wide, 128), wide)
-
-    done = [g0, g1, g2, g3, g4, g5]
-    first_r, first_l, second = [], [], []
-    for b in range(SUBS):
-        part = slice(b * wide, (b + 1) * wide)
-        mine = cols_of(tx, b)
-        out_ref[:, mine] = (total[:, part] + term(opposite, part)).astype(BF16)
-        i = 6 + 6 * b
-        first_r.append(push(out_ref.at[low, mine], i, right))
-        first_l.append(push(out_ref.at[high, mine], i + 1, left))
-        second.append(push(out_ref.at[high, mine], i + 2, right))
-        second.append(push(out_ref.at[low, mine], i + 3, left))
-    for b in range(SUBS):
-        i = 6 + 6 * b
-        first_r[b].wait_recv()
-        second.append(push(out_ref.at[low, cols_of(left, b)], i + 4, right))
-        first_l[b].wait_recv()
-        second.append(push(out_ref.at[high, cols_of(right, b)], i + 5, left))
-    for copy in second:
+    for e in range(4):
+        rest_to_mate[2][e].wait_recv()
+
+    def cols_of(owner):
+        return pl.ds(pl.multiple_of(owner * DC, 128), DC)
+
+    outs_r, outs_l, outs_far = [], [], []
+    for v in halves:
+        if v == 1:
+            total[rows_of[1]] += term(left, rows_of[1]) + term(right, rows_of[1])
+        heads_far[2 * v].wait_recv()
+        heads_far[2 * v + 1].wait_recv()
+        gathered[rows_of[v], cols_of(tx)] = (total[rows_of[v]] + term(opposite, rows_of[v])).astype(BF16)
+        mine = gathered.at[span_of[v], cols_of(tx)]
+        outs_r.append(push(mine, 8 + 4 * v, right))
+        outs_l.append(push(mine, 9 + 4 * v, left))
+
+    def place(owner):
+        rows = jnp.dot(unpick[...], gathered[:, cols_of(owner)], preferred_element_type=F32)
+        out_ref[:, cols_of(owner)] = rows.astype(BF16)
+
+    for v in halves:
+        outs_r[v].wait_recv()
+        outs_far.append(push(gathered.at[to_right[v], cols_of(left)], 10 + 4 * v, right))
+        outs_l[v].wait_recv()
+        outs_far.append(push(gathered.at[to_left[v], cols_of(right)], 11 + 4 * v, left))
+        if v == 0:
+            place(tx)
+    place(left)
+    place(right)
+    for copy in outs_far:
         copy.wait_recv()
-    for copy in done + first_r + first_l + second:
+    place(opposite)
+    for copy in pushed:
         copy.wait_send()
-    for copy in [far_a, far_b, pass_a, pass_b] + near_a + near_b + sum(spread, []) + to_mate + rest_to_mate:
+    for copy in [far_a, far_b, pass_a, pass_b] + near_a + near_b + sum(spread + rest_to_mate, []) + to_mate:
         copy.wait_send()
     some = pl.ds(0, R - 1)
     settle(meta_out.at[some], meta_send)
@@ -518,9 +545,14 @@
     out = pl.pallas_call(
         functools.partial(kernel, (R, T, S, NQ, D, KC)),
         out_shape=pltpu.VMEM((M, D), BF16),
-        in_specs=[smem, smem, smem, pl.BlockSpec(memory_space=pltpu.VMEM)] + [any_spec] * 6,
+        in_specs=[any_spec, any_spec, any_spec] + [any_spec] * 7,
         out_specs=pl.BlockSpec(memory_space=pltpu.VMEM),
         scratch_shapes=[
+            pltpu.SMEM((R,), jnp.int32),
+            pltpu.SMEM((R,), jnp.int32),
+            pltpu.SMEM((pages // R, R), jnp.int32),
+            pltpu.VMEM((1, D), F32),
+            dma((4,)),
             pltpu.VMEM((M, D), BF16),
             pltpu.VMEM((D, NQ * HD), BF16),
             pltpu.VMEM((D, HD), BF16),
@@ -533,8 +565,9 @@
             pltpu.SMEM((R, 128), jnp.int32),
             pltpu.VMEM((R, 8, 128), jnp.int32),
             pltpu.VMEM((R, 8, 128), jnp.int32),
-            pltpu.VMEM((NQ * M, R * MSG), BF16),
-            pltpu.VMEM((NQ * M, HD), F32),
+            pltpu.VMEM((NQ * GROUP * S, GROUP * MSG), BF16),
+            pltpu.VMEM((M, M), BF16),
+            pltpu.VMEM((M, D), BF16),
             pltpu.VMEM((NH * M, HD), BF16),
             pltpu.VMEM((R, MSG, HD), BF16),
             pltpu.VMEM((R, MSG, HD), BF16),
@@ -543,7 +576,7 @@
             pltpu.VMEM((T, M, NQ * HD), BF16),
             pltpu.VMEM((M, DC), F32),
             dma, dma((D // KC, 3)), dma((4,)), dma, dma,
-            dma, dma, dma, dma((R,)), dma, dma((R,)), dma((6 + 6 * SUBS,)), dma((6 + 6 * SUBS,)), dma((26,)), dma((26,)),
+            dma, dma, dma, dma((R,)), dma, dma((R,)), dma((16,)), dma((16,)), dma((38,)), dma((38,)),
         ],
         compiler_params=pltpu.CompilerParams(
             collective_id=0, has_side_effects=True, vmem_limit_bytes=58 * 1024 * 1024

time: 52.1 us -> 51.4 us (0.987)
  Pallas kernels: 50.8 us -> 50.2 us
    pallas_call x1, Pallas kernels: 50.8 us -> 50.2 us  [shards(): pl.pallas_call(functools.partial(kernel, (R, T, S, NQ, D, KC)), out_shape...]
where the time goes in v8:
time: 51.4 us; the launch traced here: 51.3 us
  Pallas kernels  50.2 us (98%)
  local copies, waits for them, and re-layouts  1.06 us (2%)
    pallas_call x1, Pallas kernels, shards(): pl.pallas_call(functools.partial(kernel, (R, T, S, NQ, D, KC)), out_shape...  50.2 us
    unnamed x1, local copies, waits for them, and re-layouts  1.06 us

profile of v8, /device:TPU:0, one launch (start us, length us, event | category | flops | bytes accessed | tf_op | source)
XLA Modules:
  0.0 51.3 jit_solution(15751649876465951230)
XLA Ops:
  0.0 50.2 %decode_attention.1 = bf16[128,5120]{1,0:T(8,128)(2,1)S(1)} custom-call(s32[32]{0:T(128)} %dest_hbm.1, s32[32]{0:T(128)} %len_hbm.1, s32[4,32]{1,0:T(4,128)} %bitcast.7, f32[1,5120]{1,0:T(1,128)} %bitcast.6, bf16[128,5120]{1,0:T(8,128)(2,1)} %bitcast.5, bf16[5120,640]{1,0:T(8,128)(2,1)} %wq_hbm.1, bf16[5120,128]{1,0:T(8,128)(2,1)} %wk_hbm.1, ...), custom_call_target="tpu_custom_call" | custom-call | tf_op jit(solution)/shard_map/decode_attention/pallas_call | solution.py:545
  50.2 1.1 %copy.12 = bf16[4,32,5120]{2,1,0:T(8,128)(2,1)} copy(bf16[4,32,5120]{2,1,0:T(8,128)(2,1)S(1)} %bitcast.4) | data formatting | bytes 2621440

commit v9 on v7

--- a/solution.py
+++ b/solution.py
@@ -30,8 +30,9 @@
 
 def kernel(
     sizes,
-    dest_sm, len_sm, table_sm, gain_ref, hid_hbm, wq_hbm, wk_hbm, wv_hbm, wo_hbm, kv_hbm,
+    dest_hbm, len_hbm, table_hbm, gain_hbm, hid_hbm, wq_hbm, wk_hbm, wv_hbm, wo_hbm, kv_hbm,
     out_ref,
+    dest_sm, len_sm, table_sm, gain_ref, small_sem,
     hid, wq, wk, wv, kv, wf, relay, acc, code, code_sm, meta_out, meta_in, unpick, by_head, stack,
     q_out, q_in, h_out, h_in, heads, total,
     hid_sem, w_sem, kv_sem, wo_sem, code_sem,
@@ -121,6 +122,14 @@
             pltpu.make_async_copy(wv_hbm.at[rows], wv.at[rows], w_sem.at[c, 2]),
         )
 
+    small = [
+        pltpu.make_async_copy(src, dst, small_sem.at[i])
+        for i, (src, dst) in enumerate(
+            ((dest_hbm, dest_sm), (len_hbm, len_sm), (gain_hbm, gain_ref), (table_hbm, table_sm))
+        )
+    ]
+    for copy in small:
+        copy.start()
     hid_copy = pltpu.make_async_copy(hid_hbm, hid, hid_sem)
     hid_copy.start()
     def load(c):
@@ -128,8 +137,6 @@
             for copy in weight_copies(c):
                 copy.start()
 
-    load(0)
-
     barrier = pltpu.get_barrier_semaphore()
 
     def far_first(k):
@@ -140,12 +147,15 @@
         pl.semaphore_signal(barrier, inc=1, device_id={"replica": n}, device_id_type=MESH)
         return carry
 
-    lax.fori_loop(0, R - 1, greet, 0)
+    lax.fori_loop(0, R - 1, greet, 0, unroll=True)
     for other in (right, left):
         pl.semaphore_signal(barrier, inc=1, device_id={"tensor": other}, device_id_type=MESH)
 
+    load(0)
     load(1)
 
+    small[0].wait()
+    small[1].wait()
     numbers = lax.broadcasted_iota(jnp.int32, (R, 128), 0)
     codes = jnp.zeros((R, 128), jnp.int32)
     for b in range(R):
@@ -180,11 +190,12 @@
         meta_copy(mod(me + far_first(k), R)).start()
         return carry
 
-    lax.fori_loop(0, R - 1, send_meta, 0)
+    lax.fori_loop(0, R - 1, send_meta, 0, unroll=True)
     far_a.start()
     far_b.start()
 
     hid_copy.wait()
+    small[2].wait()
     load(2)
     squares = jnp.zeros((M, 128), F32)
     for c in range(D // 128):
@@ -320,6 +331,7 @@
     far_b.wait_recv()
     pass_b.start()
     code_copy.wait()
+    small[3].wait()
     for copy in kv_copies:
         copy.wait()
 
@@ -391,7 +403,7 @@
 
         return carry
 
-    lax.fori_loop(0, groups, attend_group, 0, unroll=2)
+    lax.fori_loop(0, groups, attend_group, 0, unroll=4)
     h_in[me] = h_out[me]
     share_near(0)
     share_near(1)
@@ -518,9 +530,14 @@
     out = pl.pallas_call(
         functools.partial(kernel, (R, T, S, NQ, D, KC)),
         out_shape=pltpu.VMEM((M, D), BF16),
-        in_specs=[smem, smem, smem, pl.BlockSpec(memory_space=pltpu.VMEM)] + [any_spec] * 6,
+        in_specs=[any_spec, any_spec, any_spec] + [any_spec] * 7,
         out_specs=pl.BlockSpec(memory_space=pltpu.VMEM),
         scratch_shapes=[
+            pltpu.SMEM((R,), jnp.int32),
+            pltpu.SMEM((R,), jnp.int32),
+            pltpu.SMEM((pages // R, R), jnp.int32),
+            pltpu.VMEM((1, D), F32),
+            dma((4,)),
             pltpu.VMEM((M, D), BF16),
             pltpu.VMEM((D, NQ * HD), BF16),
             pltpu.VMEM((D, HD), BF16),

time: 52.1 us -> 50.9 us (0.977)
  Pallas kernels: 50.8 us -> 49.7 us
    pallas_call x1, Pallas kernels: 50.8 us -> 49.7 us  [shards(): pl.pallas_call(functools.partial(kernel, (R, T, S, NQ, D, KC)), out_shape...]
where the time goes in v9:
time: 50.9 us; the launch traced here: 50.8 us
  Pallas kernels  49.7 us (98%)
  local copies, waits for them, and re-layouts  1.06 us (2%)
    pallas_call x1, Pallas kernels, shards(): pl.pallas_call(functools.partial(kernel, (R, T, S, NQ, D, KC)), out_shape...  49.7 us
    unnamed x1, local copies, waits for them, and re-layouts  1.06 us

profile of v9, /device:TPU:0, one launch (start us, length us, event | category | flops | bytes accessed | tf_op | source)
XLA Modules:
  0.0 50.8 jit_solution(12229678178764903649)
XLA Ops:
  0.0 49.7 %decode_attention.1 = bf16[128,5120]{1,0:T(8,128)(2,1)S(1)} custom-call(s32[32]{0:T(128)} %dest_hbm.1, s32[32]{0:T(128)} %len_hbm.1, s32[4,32]{1,0:T(4,128)} %bitcast.7, f32[1,5120]{1,0:T(1,128)} %bitcast.6, bf16[128,5120]{1,0:T(8,128)(2,1)} %bitcast.5, bf16[5120,640]{1,0:T(8,128)(2,1)} %wq_hbm.1, bf16[5120,128]{1,0:T(8,128)(2,1)} %wk_hbm.1, ...), custom_call_target="tpu_custom_call" | custom-call | tf_op jit(solution)/shard_map/decode_attention/pallas_call | solution.py:530
  49.7 1.1 %copy.12 = bf16[4,32,5120]{2,1,0:T(8,128)(2,1)} copy(bf16[4,32,5120]{2,1,0:T(8,128)(2,1)S(1)} %bitcast.4) | data formatting | bytes 2621440

commit v10 on v9

--- a/solution.py
+++ b/solution.py
@@ -453,19 +453,19 @@
         return jnp.dot(heads[owner], wf[rows, cols], preferred_element_type=F32)
 
     every = slice(0, DC)
-    wo_copy.wait()
-    total[...] = term(tx, every)
     for j in (0, 1):
         for e in range(4):
             spread[j][e].wait_recv()
         rest_to_mate[j].start()
-    for e in range(4):
-        spread[2][e].wait_recv()
-    rest_to_mate[2].start()
+    wo_copy.wait()
+    total[...] = term(tx, every)
     g0.wait_recv()
     g4 = push(heads.at[left, low], 4, right)
     g1.wait_recv()
     g5 = push(heads.at[right, high], 5, left)
+    for e in range(4):
+        spread[2][e].wait_recv()
+    rest_to_mate[2].start()
     g2.wait_recv()
     to_mate[0].wait_recv()
     rest_to_mate[0].wait_recv()

time: 50.9 us -> 50.3 us (0.988)
  Pallas kernels: 49.7 us -> 49.1 us
    pallas_call x1, Pallas kernels: 49.7 us -> 49.1 us  [shards(): pl.pallas_call(functools.partial(kernel, (R, T, S, NQ, D, KC)), out_shape...]
where the time goes in v10:
time: 50.3 us; the launch traced here: 50.2 us
  Pallas kernels  49.1 us (98%)
  local copies, waits for them, and re-layouts  1.06 us (2%)
    pallas_call x1, Pallas kernels, shards(): pl.pallas_call(functools.partial(kernel, (R, T, S, NQ, D, KC)), out_shape...  49.1 us
    unnamed x1, local copies, waits for them, and re-layouts  1.06 us

profile of v10, /device:TPU:0, one launch (start us, length us, event | category | flops | bytes accessed | tf_op | source)
XLA Modules:
  0.0 50.2 jit_solution(12931208608287301318)
XLA Ops:
  0.0 49.1 %decode_attention.1 = bf16[128,5120]{1,0:T(8,128)(2,1)S(1)} custom-call(s32[32]{0:T(128)} %dest_hbm.1, s32[32]{0:T(128)} %len_hbm.1, s32[4,32]{1,0:T(4,128)} %bitcast.7, f32[1,5120]{1,0:T(1,128)} %bitcast.6, bf16[128,5120]{1,0:T(8,128)(2,1)} %bitcast.5, bf16[5120,640]{1,0:T(8,128)(2,1)} %wq_hbm.1, bf16[5120,128]{1,0:T(8,128)(2,1)} %wk_hbm.1, ...), custom_call_target="tpu_custom_call" | custom-call | tf_op jit(solution)/shard_map/decode_attention/pallas_call | solution.py:530
  49.1 1.1 %copy.12 = bf16[4,32,5120]{2,1,0:T(8,128)(2,1)} copy(bf16[4,32,5120]{2,1,0:T(8,128)(2,1)S(1)} %bitcast.4) | data formatting | bytes 2621440

commit v11 on v10

--- a/solution.py
+++ b/solution.py
@@ -474,20 +474,22 @@
     to_mate[1].wait_recv()
     rest_to_mate[1].wait_recv()
     total[...] += term(right, every)
-    to_mate[2].wait_recv()
-    rest_to_mate[2].wait_recv()
     g4.wait_recv()
     g5.wait_recv()
 
     wide = DC // SUBS
 
     def cols_of(owner, b):
-        return pl.ds(pl.multiple_of(owner * DC + b * wide, 128), wide)
+        own = core if b == 0 else 1 - core
+        return pl.ds(pl.multiple_of(owner * DC + own * wide, 128), wide)
 
     done = [g0, g1, g2, g3, g4, g5]
     first_r, first_l, second = [], [], []
     for b in range(SUBS):
-        part = slice(b * wide, (b + 1) * wide)
+        part = cols_of(0, b)
+        if b == 1:
+            to_mate[2].wait_recv()
+            rest_to_mate[2].wait_recv()
         mine = cols_of(tx, b)
         out_ref[:, mine] = (total[:, part] + term(opposite, part)).astype(BF16)
         i = 6 + 6 * b

time: 50.3 us -> 50.2 us (level)
  no operation moved by 1% of the time
where the time goes in v11:
time: 50.2 us; the launch traced here: 49.9 us
  Pallas kernels  48.9 us (97%)
  local copies, waits for them, and re-layouts  1.06 us (2%)
    pallas_call x1, Pallas kernels, shards(): pl.pallas_call(functools.partial(kernel, (R, T, S, NQ, D, KC)), out_shape...  48.9 us
    unnamed x1, local copies, waits for them, and re-layouts  1.06 us

profile of v11, /device:TPU:0, one launch (start us, length us, event | category | flops | bytes accessed | tf_op | source)
XLA Modules:
  0.0 49.9 jit_solution(14760224363004540526)
XLA Ops:
  0.0 48.9 %decode_attention.1 = bf16[128,5120]{1,0:T(8,128)(2,1)S(1)} custom-call(s32[32]{0:T(128)} %dest_hbm.1, s32[32]{0:T(128)} %len_hbm.1, s32[4,32]{1,0:T(4,128)} %bitcast.7, f32[1,5120]{1,0:T(1,128)} %bitcast.6, bf16[128,5120]{1,0:T(8,128)(2,1)} %bitcast.5, bf16[5120,640]{1,0:T(8,128)(2,1)} %wq_hbm.1, bf16[5120,128]{1,0:T(8,128)(2,1)} %wk_hbm.1, ...), custom_call_target="tpu_custom_call" | custom-call | tf_op jit(solution)/shard_map/decode_attention/pallas_call | solution.py:532
  48.9 1.1 %copy.12 = bf16[4,32,5120]{2,1,0:T(8,128)(2,1)} copy(bf16[4,32,5120]{2,1,0:T(8,128)(2,1)S(1)} %bitcast.4) | data formatting | bytes 2621440
